TPU v7x, 32 devices: a whole 2x2x4 slice. The times are simulated.
32 devices in a mesh: chan: 4 (over z), tm: 8 (over y, x, core).
Axes of the slice: x: 2, y: 2, z: 4, core: 2. Of those that a mesh axis runs over, the one named last changes fastest.
Arguments:
- symbols: int32 [32, 65536], P('chan', 'tm'), may hold values from 0 to 63
- incidence: int32 [128, 6], P('chan'), may hold values from 0 to 31, as said below
- delays: int32 [128, 6], P('chan'), may hold values from 0 to 63
- gains: float32 [2, 128, 6], P(None, 'chan'), may hold values from -4 to 4
- echoes: bfloat16 [2, 128, 65536], P(None, 'chan', 'tm'), may hold values from -6 to 6
Outputs:
- cancelled: bfloat16 [2, 128, 65536], P(None, 'chan', 'tm')
- weights: float32 [2, 128, 384], P(None, 'chan')
Inputs may be any that keep to these rules, and one draw needn't show every extreme that they name: `incidence`: row r names 6 distinct illuminators, all owned by chan index c = r // 32 or the next index c + 1 taken cyclically: ids from c * 8 to (c + 2) * 8 - 1, modulo 32.
All inputs are finite; a program needn't handle non-finite values.
Results may differ from a plain program's by a relative error of at most 0.024.
Values may be sent and summed in bfloat16 or wider, within the bound.
A program may use at most 128 MiB of HBM per device.

v0:
```python
import math

import jax
import jax.numpy as jnp
from jax import lax
from jax.sharding import PartitionSpec as P

ACTIVE = 6817
DELAYS = 64
PER_RECV = 6


loading = 0.1
batch_rows = 8
HIGHEST = lax.Precision.HIGHEST


def passed_along(array, axis, by):
    peers = lax.axis_size(axis)
    return lax.ppermute(array, axis, [(i, (i + by) % peers) for i in range(peers)])


def from_behind(block, axis, distance):
    devices = range(lax.axis_size(axis))
    route = [(i - distance, i) for i in devices if i - distance in devices]
    return lax.ppermute(block, axis, route)


def rotation_angle_grid(row_count, col_count, period):
    product = (
        jnp.arange(row_count, dtype=jnp.int32)[:, None]
        * jnp.arange(col_count, dtype=jnp.int32)[None, :]
    )
    phases = (product % period).astype(jnp.float32) * (2.0 * math.pi / period)
    return (jnp.cos(phases), jnp.sin(phases))


def complex_multiply_result(pattern, left_pair, right_pair):
    real_part = jnp.einsum(pattern, left_pair[0], right_pair[0], precision=HIGHEST) - jnp.einsum(
        pattern, left_pair[1], right_pair[1], precision=HIGHEST
    )
    imag_part = jnp.einsum(pattern, left_pair[0], right_pair[1], precision=HIGHEST) + jnp.einsum(
        pattern, left_pair[1], right_pair[0], precision=HIGHEST
    )
    return (real_part, imag_part)


def remodulate(symbols):
    emitter_number, length = symbols.shape
    column_entries = 128
    increment_spacing = length // column_entries
    inphase_amplitude = (2 * (symbols % 8) - 7).astype(jnp.float32) / math.sqrt(42.0)
    quadrature_amplitude = (2 * (symbols // 8) - 7).astype(jnp.float32) / math.sqrt(42.0)
    subcarrier = jnp.arange(length, dtype=jnp.int32) - length // 2
    occupied_tones = (jnp.abs(subcarrier) <= (ACTIVE - 1) // 2).astype(jnp.float32)
    tone_symbols = (
        (inphase_amplitude * occupied_tones).reshape(
            emitter_number, increment_spacing, column_entries
        ),
        (quadrature_amplitude * occupied_tones).reshape(
            emitter_number, increment_spacing, column_entries
        ),
    )
    partial_result = complex_multiply_result(
        "mb,nbd->nmd",
        rotation_angle_grid(increment_spacing, increment_spacing, increment_spacing),
        tone_symbols,
    )
    twiddle = rotation_angle_grid(increment_spacing, column_entries, length)
    partial_result = (
        partial_result[0] * twiddle[0] - partial_result[1] * twiddle[1],
        partial_result[0] * twiddle[1] + partial_result[1] * twiddle[0],
    )
    frequency_spectrum = complex_multiply_result(
        "pho,oj->phj",
        partial_result,
        rotation_angle_grid(column_entries, column_entries, column_entries),
    )
    alternate = (1 - 2 * (jnp.arange(length, dtype=jnp.int32) % 2)).astype(jnp.float32) / math.sqrt(
        ACTIVE
    )
    real_part = (
        jnp.swapaxes(frequency_spectrum[0], 1, 2).reshape(emitter_number, length) * alternate
    )
    imag_part = (
        jnp.swapaxes(frequency_spectrum[1], 1, 2).reshape(emitter_number, length) * alternate
    )
    return jnp.stack([real_part, imag_part], axis=1).astype(jnp.bfloat16)


def lag_table(lag_count):
    spread = jnp.arange(2 * lag_count, dtype=jnp.int32)[:, None, None]
    column = jnp.arange(lag_count, dtype=jnp.int32)[None, :, None]
    lag_pos = jnp.arange(lag_count, dtype=jnp.int32)[None, None, :]
    return (spread == lag_count + column - lag_pos).astype(jnp.float32)


def lag_sums(outer):
    leading = outer.shape[:-2]
    lag_count = outer.shape[-2]
    width = outer.shape[-1]
    flat = outer.reshape(leading + (lag_count * width,))
    flat = jnp.pad(flat, [(0, 0)] * len(leading) + [(0, lag_count)])
    skewed = flat.reshape(leading + (lag_count, width + 1))[..., 1 : lag_count + 1]
    return jnp.flip(jnp.sum(skewed, axis=-2), axis=-1)


def toeplitz_tables(lag_count):
    row_pos = jnp.arange(lag_count, dtype=jnp.int32)[:, None, None]
    col_pos = jnp.arange(lag_count, dtype=jnp.int32)[None, :, None]
    lag_pos = jnp.arange(lag_count, dtype=jnp.int32)[None, None, :]
    lower_part = (row_pos - col_pos == lag_pos).astype(jnp.float32)
    upper_part = ((col_pos - row_pos == lag_pos) & (lag_pos > 0)).astype(jnp.float32)
    return (lower_part, upper_part)


def banded_apply(looked, banded):
    real_part = jnp.einsum(
        "bkqv,bkvp->bqp", looked[:, :, 0], banded[0], preferred_element_type=jnp.float32
    ) - jnp.einsum("bkqv,bkvp->bqp", looked[:, :, 1], banded[1], preferred_element_type=jnp.float32)
    imag_part = jnp.einsum(
        "bkqv,bkvp->bqp", looked[:, :, 0], banded[1], preferred_element_type=jnp.float32
    ) + jnp.einsum("bkqv,bkvp->bqp", looked[:, :, 1], banded[0], preferred_element_type=jnp.float32)
    return (real_part, imag_part)


def local(symbols, incidence, delays, gains, echoes):
    local_refs = remodulate(symbols)
    owned = local_refs.shape[0]
    length = local_refs.shape[2]
    lag_count = DELAYS
    taps_count = PER_RECV * DELAYS
    chan_count = lax.axis_size("chan")
    chan_index = lax.axis_index("chan")
    window_count = 2 * owned
    following = passed_along(local_refs, "chan", -1)
    window = jnp.concatenate([local_refs, following], axis=0)
    previous = from_behind(window[:, :, length - lag_count :], "tm", 1)
    extended = jnp.concatenate([previous, window], axis=2)
    block_count = length // lag_count
    pieces = extended.reshape(window_count, 2, block_count + 1, lag_count)
    frames = jnp.concatenate([pieces[:, :, :-1], pieces[:, :, 1:]], axis=3)
    current = pieces[:, :, 1:]
    tm_count = lax.axis_size("tm")
    tm_index = lax.axis_index("tm")
    scale = 1.0 / (length * tm_count)
    diagonal_table = lag_table(lag_count)
    lag_range = jnp.arange(lag_count, dtype=jnp.int32)

    def pair_row(frame):
        real_part = jnp.einsum(
            "qv,jqp->jpv", frame[0], current[:, 0], preferred_element_type=jnp.float32
        ) + jnp.einsum("qv,jqp->jpv", frame[1], current[:, 1], preferred_element_type=jnp.float32)
        imag_part = jnp.einsum(
            "qv,jqp->jpv", frame[0], current[:, 1], preferred_element_type=jnp.float32
        ) - jnp.einsum("qv,jqp->jpv", frame[1], current[:, 0], preferred_element_type=jnp.float32)
        return jnp.concatenate([lag_sums(real_part), lag_sums(imag_part)], axis=1)

    corr_part = lax.map(pair_row, frames) * scale
    owner_chan = incidence // owned
    slot = (owner_chan - chan_index) % chan_count * owned + incidence % owned
    recv_count = echoes.shape[1]
    group_count = recv_count // batch_rows

    def first_pass(step, carry):
        received_all, cross_all = carry
        start = step * batch_rows
        slots = lax.dynamic_slice_in_dim(slot, start, batch_rows, 0).reshape(-1)
        lag_values = lax.dynamic_slice_in_dim(delays, start, batch_rows, 0)
        gain = lax.dynamic_slice_in_dim(gains, start, batch_rows, 1)
        echo = lax.dynamic_slice_in_dim(echoes, start, batch_rows, 1)
        looked = jnp.take(frames, slots, axis=0).reshape(
            batch_rows, PER_RECV, 2, block_count, 2 * lag_count
        )
        onehot = (lag_values[:, :, None] == lag_range[None, None, :]).astype(jnp.float32)
        gain_taps = gain[:, :, :, None] * onehot[None]
        band = jnp.einsum("vpa,xbka->xbkvp", diagonal_table, gain_taps, precision=HIGHEST)
        band_high = band.astype(jnp.bfloat16)
        band_low = (band - band_high.astype(jnp.float32)).astype(jnp.bfloat16)
        high_re, high_im = banded_apply(looked, band_high)
        low_re, low_im = banded_apply(looked, band_low)
        direct_re = (high_re + low_re).reshape(batch_rows, length)
        direct_im = (high_im + low_im).reshape(batch_rows, length)
        received = jnp.stack(
            [echo[0].astype(jnp.float32) + direct_re, echo[1].astype(jnp.float32) + direct_im]
        ).astype(jnp.bfloat16)
        signal = received.reshape(2, batch_rows, block_count, lag_count)
        real_part = jnp.einsum(
            "bkqv,bqp->bkpv", looked[:, :, 0], signal[0], preferred_element_type=jnp.float32
        ) + jnp.einsum(
            "bkqv,bqp->bkpv", looked[:, :, 1], signal[1], preferred_element_type=jnp.float32
        )
        imag_part = jnp.einsum(
            "bkqv,bqp->bkpv", looked[:, :, 0], signal[1], preferred_element_type=jnp.float32
        ) - jnp.einsum(
            "bkqv,bqp->bkpv", looked[:, :, 1], signal[0], preferred_element_type=jnp.float32
        )
        cross_re = lag_sums(real_part).reshape(batch_rows, taps_count)
        cross_im = lag_sums(imag_part).reshape(batch_rows, taps_count)
        cross_piece = jnp.stack([cross_re, cross_im]) * scale
        received_all = lax.dynamic_update_slice_in_dim(received_all, received, start, 1)
        cross_all = lax.dynamic_update_slice_in_dim(cross_all, cross_piece, start, 1)
        return (received_all, cross_all)

    received_init = jnp.zeros((2, recv_count, length), jnp.bfloat16)
    cross_init = jnp.zeros((2, recv_count, taps_count), jnp.float32)
    received_all, cross_all = lax.fori_loop(0, group_count, first_pass, (received_init, cross_init))
    share = recv_count // tm_count
    corr, cross_whole = lax.psum((corr_part, cross_all), "tm")
    cross = lax.dynamic_slice_in_dim(cross_whole, tm_index * share, share, 1)
    mine = lax.dynamic_slice_in_dim(slot, tm_index * share, share, 0)
    selector = (
        mine[:, :, None] == jnp.arange(window_count, dtype=jnp.int32)[None, None, :]
    ).astype(jnp.float32)
    gathered = jnp.einsum("rkw,wvd,rlv->rkld", selector, corr, selector, precision=HIGHEST)
    lower_part, upper_part = toeplitz_tables(lag_count)
    sub_re = gathered[..., :lag_count]
    sub_im = gathered[..., lag_count:]
    gram_re = jnp.einsum("rkld,abd->rkalb", sub_re, lower_part, precision=HIGHEST) + jnp.einsum(
        "rlkd,abd->rkalb", sub_re, upper_part, precision=HIGHEST
    )
    gram_im = jnp.einsum("rkld,abd->rkalb", sub_im, lower_part, precision=HIGHEST) - jnp.einsum(
        "rlkd,abd->rkalb", sub_im, upper_part, precision=HIGHEST
    )
    gram_re = gram_re.reshape(share, taps_count, taps_count) + loading * jnp.eye(
        taps_count, dtype=jnp.float32
    )
    gram_im = gram_im.reshape(share, taps_count, taps_count)
    system = jnp.concatenate(
        [jnp.concatenate([gram_re, -gram_im], axis=2), jnp.concatenate([gram_im, gram_re], axis=2)],
        axis=1,
    )
    factor = jnp.linalg.cholesky(system)
    right_side = jnp.concatenate([cross[0], cross[1]], axis=1)
    solved = jax.vmap(
        lambda chol_factor, vector: jax.scipy.linalg.cho_solve((chol_factor, True), vector)
    )(factor, right_side)
    local_weights = jnp.stack([solved[:, :taps_count], solved[:, taps_count:]])
    weights = lax.all_gather(local_weights, "tm", axis=1, tiled=True)
    taps = weights.astype(jnp.bfloat16).reshape(2, recv_count, PER_RECV, lag_count)
    table_half = diagonal_table.astype(jnp.bfloat16)

    def second_pass(step, cancelled_all):
        start = step * batch_rows
        slots = lax.dynamic_slice_in_dim(slot, start, batch_rows, 0).reshape(-1)
        looked = jnp.take(frames, slots, axis=0).reshape(
            batch_rows, PER_RECV, 2, block_count, 2 * lag_count
        )
        tap_rows = lax.dynamic_slice_in_dim(taps, start, batch_rows, 1)
        banded = jnp.einsum(
            "vpa,xbka->xbkvp", table_half, tap_rows, preferred_element_type=jnp.float32
        ).astype(jnp.bfloat16)
        proj_re, proj_im = banded_apply(looked, banded)
        received = lax.dynamic_slice_in_dim(received_all, start, batch_rows, 1).astype(jnp.float32)
        result = jnp.stack(
            [
                received[0] - proj_re.reshape(batch_rows, length),
                received[1] - proj_im.reshape(batch_rows, length),
            ]
        ).astype(jnp.bfloat16)
        return lax.dynamic_update_slice_in_dim(cancelled_all, result, start, 1)

    cancelled = lax.fori_loop(
        0, group_count, second_pass, jnp.zeros((2, recv_count, length), jnp.bfloat16)
    )
    return (cancelled, weights)


def solution(mesh):
    in_specs = (
        P("chan", "tm"),
        P("chan", None),
        P("chan", None),
        P(None, "chan", None),
        P(None, "chan", "tm"),
    )
    out_specs = (P(None, "chan", "tm"), P(None, "chan", None))
    return jax.shard_map(local, mesh=mesh, in_specs=in_specs, out_specs=out_specs, check_vma=False)
```

profile of v0, /device:TPU:0, one launch (start us, length us, event | category | flops | bytes accessed | tf_op | source)
XLA Modules:
  0.0 1361.7 jit_solution(8024505355895959593)
XLA Ops:
  30.3 95.9 %while.45 = (s32[]{:T(128)}, f32[16,16,128]{2,0,1:T(8,128)S(1)}, bf16[16,2,128,128]{3,2,1,0:T(8,128)(2,1)S(1)}, bf16[16,2,128,64]{2,3,0,1:T(8,128)(2,1)}, s32[]{:T(128)}, /*index=5*/s32[]{:T(128)}, s32[]{}, f32[]{:T(128)}) while((s32[]{:T(128)}, f32[16,16,128]{2,0,1:T(8,128)S(1)}, bf16[16,2,128,128]{3,2,1,0:T(8,128)(2,1)S(1)}, ...), condition=%wide.region_3.4_spmd, body=%wide.region_0.3_spmd.sunk | while | flops 134610944 | bytes 14368901 | solution.py:159
  128.6 204.1 %while.47 = (s32[]{:T(128)}, bf16[2,32,8192]{2,1,0:T(8,128)(2,1)}, f32[2,32,384]{2,1,0:T(8,128)}, bf16[2,32,8192]{2,1,0:T(8,128)(2,1)}, s32[32,6]{1,0:T(8,128)S(...) while((s32[]{:T(128)}, bf16[2,32,8192]{2,1,0:T(8,128)(2,1)}, ...), condition=%wide.region_20.22_spmd.clone, body=%wide.region_17.21_spmd.clone.sunk | while | flops 1820216704 | bytes 142557776 | solution.py:207
  333.3 56.6 %all-reduce.8.cloned.1.call-done = (f32[2,32,384]{2,1,0:T(8,128)}, f32[16,16,128]{2,0,1:T(8,128)}) async-done(((f32[2,32,384]{2,1,0:T(8,128)}, f32[16,16,128]{2,0,1:T(8,128)}), (f32[2,32,384]{2,1,0:T(8,128)}, f32[16,16,128]{2,0,1:T(8,128)})) %all-reduce.8.cloned.1.call-update) | async-done | bytes 229392 | tf_op jit(solution)/shard_map/psum | solution.py:209
  404.8 7.0 copy.328
  417.9 6.8 bitcast_add_fusion.1
  424.7 6.9 copy.316
  444.9 9.7 copy.226
  454.6 6.5 fusion.66
  464.7 47.1 %custom-call.56 = f32[4,128,128]{2,1,0:T(8,128)S(1)} custom-call(f32[4,128,128]{2,1,0:T(8,128)S(1)} %cholesky.426), custom_call_target="Cholesky" | custom-call | tf_op jit(solution)/shard_map/jit(cholesky)/cholesky | solution.py:233
  516.3 39.3 %custom-call.57 = f32[4,1,128,128]{2,3,1,0:T(8,128)S(1)} custom-call(f32[4,1,128,128]{3,2,1,0:T(8,128)S(1)} %select_bitcast_fusion.4), custom_call_target="InvertDiagBlocksLowerTriangular" | custom-call | tf_op jit(solution)/shard_map/jit(cholesky)/cholesky | solution.py:233
  562.0 47.1 %custom-call.58 = f32[4,128,128]{2,1,0:T(8,128)S(1)} custom-call(f32[4,128,128]{2,1,0:T(8,128)S(1)} %cholesky.430), custom_call_target="Cholesky" | custom-call | tf_op jit(solution)/shard_map/jit(cholesky)/cholesky | solution.py:233
  609.9 39.3 %custom-call.59 = f32[4,1,128,128]{2,3,1,0:T(8,128)S(1)} custom-call(f32[4,1,128,128]{3,2,1,0:T(8,128)S(1)} %get-tuple-element.643), custom_call_target="InvertDiagBlocksLowerTriangular" | custom-call | tf_op jit(solution)/shard_map/jit(cholesky)/cholesky | solution.py:233
  655.3 47.1 %custom-call.60 = f32[4,128,128]{2,1,0:T(8,128)S(1)} custom-call(f32[4,128,128]{2,1,0:T(8,128)S(1)} %cholesky.435), custom_call_target="Cholesky" | custom-call | tf_op jit(solution)/shard_map/jit(cholesky)/cholesky | solution.py:233
  703.3 39.3 %custom-call.61 = f32[4,1,128,128]{2,3,1,0:T(8,128)S(1)} custom-call(f32[4,1,128,128]{3,2,1,0:T(8,128)S(1)} %get-tuple-element.641), custom_call_target="InvertDiagBlocksLowerTriangular" | custom-call | tf_op jit(solution)/shard_map/jit(cholesky)/cholesky | solution.py:233
  748.9 47.4 %custom-call.62 = f32[4,128,128]{2,1,0:T(8,128)S(1)} custom-call(f32[4,128,128]{2,1,0:T(8,128)S(1)} %cholesky.440), custom_call_target="Cholesky" | custom-call | tf_op jit(solution)/shard_map/jit(cholesky)/cholesky | solution.py:233
  797.0 39.3 %custom-call.63 = f32[4,1,128,128]{2,3,1,0:T(8,128)S(1)} custom-call(f32[4,1,128,128]{3,2,1,0:T(8,128)S(1)} %get-tuple-element.639), custom_call_target="InvertDiagBlocksLowerTriangular" | custom-call | tf_op jit(solution)/shard_map/jit(cholesky)/cholesky | solution.py:233
  842.5 48.5 %custom-call.64 = f32[4,128,128]{2,1,0:T(8,128)} custom-call(f32[4,128,128]{2,1,0:T(8,128)} %cholesky.445), custom_call_target="Cholesky" | custom-call | tf_op jit(solution)/shard_map/jit(cholesky)/cholesky | solution.py:233
  892.8 40.7 %custom-call.65 = f32[4,1,128,128]{2,3,1,0:T(8,128)} custom-call(f32[4,1,128,128]{3,2,1,0:T(8,128)} %get-tuple-element.637), custom_call_target="InvertDiagBlocksLowerTriangular" | custom-call | tf_op jit(solution)/shard_map/jit(cholesky)/cholesky | solution.py:233
  938.9 47.1 %custom-call.66 = f32[4,128,128]{2,1,0:T(8,128)S(1)} custom-call(f32[4,128,128]{2,1,0:T(8,128)S(1)} %fusion.103), custom_call_target="Cholesky" | custom-call | tf_op jit(solution)/shard_map/jit(cholesky)/cholesky | solution.py:233
  988.6 8.5 select_select_fusion
  997.1 22.7 %while.46 = (s32[]{:T(128)}, f32[4,768,768]{2,1,0:T(8,128)}, s32[6,2]{0,1:T(2,128)S(1)}, f32[6,4,128,128]{3,2,0,1:T(8,128)}, s32[]{:T(128)}) while((s32[]{:T(128)}, f32[4,768,768]{2,1,0:T(8,128)}, s32[6,2]{0,1:T(2,128)S(1)}, f32[6,4,128,128]{3,2,0,1:T(8,128)}, s32[]{:T(128)}) %tuple.164), condition=%wide.while_cond, body=%wide.while_body.sunk | while | flops 2 | bytes 525921 | solution.py:236
  1019.8 236.6 %custom-call.67 = f32[4,6,128,128]{2,3,1,0:T(8,128)S(1)} custom-call(f32[4,6,128,128]{3,2,1,0:T(8,128)} %bitcast.706), custom_call_target="InvertDiagBlocksLowerTriangular" | custom-call | tf_op jit(solution)/shard_map/vmap(jit(_cho_solve))/triangular_solve | solution.py:236
  1281.4 9.9 all_gather.3
  1293.9 60.6 %while.48 = (s32[]{:T(128)}, bf16[2,32,8192]{2,1,0:T(8,128)(2,1)}, bf16[2,32,8192]{2,1,0:T(8,128)(2,1)}, s32[32,6]{1,0:T(8,128)}, bf16[16,2,128,128]{3,2,1,0:T(8...) while((s32[]{:T(128)}, bf16[2,32,8192]{2,1,0:T(8,128)(2,1)}, ...), condition=%wide.region_23.25_spmd.clone, body=%wide.region_22.24_spmd.clone.sunk | while | flops 508298688 | bytes 64534532 | solution.py:263
  (850 shorter events, 511.8 us)
Async XLA Ops:
  7.2 382.7 %all-reduce.8.cloned.1.call-start = ((), (), s32[]{:S(2)}) async-start(), calls=%async_computation | async-start | bytes 458752 | tf_op jit(solution)/shard_map/psum | solution.py:209
  12.9 10.1 copy-start.19
  14.2 10.7 collective-permute-start
  24.9 2.1 collective-permute-start.1
  30.2 98.4 %copy-start.15 = (f32[2,32,6]{1,0,2:T(2,128)S(1)}, f32[2,32,6]{1,0,2:T(2,128)}, u32[]{:S(2)}) copy-start(f32[2,32,6]{1,0,2:T(2,128)} %param.16) | copy-start | bytes 4612
  30.2 98.4 %copy-start.16 = (s32[32,6]{0,1:T(8,128)S(1)}, s32[32,6]{0,1:T(8,128)}, u32[]{:S(2)}) copy-start(s32[32,6]{0,1:T(8,128)} %param.15) | copy-start | bytes 2308
  128.6 261.3 %copy-start.18 = (s32[4,6]{1,0:T(4,128)S(1)}, s32[4,6]{1,0:T(4,128)}, u32[]{:S(2)}) copy-start(s32[4,6]{1,0:T(4,128)} %constant_dynamic-slice_fusion.5) | copy-start | bytes 292
  128.6 263.4 %copy-start.13 = (s32[64,64]{1,0:T(8,128)S(1)}, s32[64,64]{1,0:T(8,128)}, u32[]{:S(2)}) copy-start(s32[64,64]{1,0:T(8,128)} %iota_subtract_fusion.1) | copy-start | bytes 49156
  134.0 5.5 copy-start.8
  139.5 3.0 copy-start
  184.9 5.5 copy-start.8
  190.4 3.0 copy-start
  235.7 5.5 copy-start.8
  241.2 3.0 copy-start
  286.6 5.5 copy-start.8
  292.1 3.0 copy-start
  394.9 4.9 copy-start.20
  437.3 3.6 copy-start.6
  461.1 3.6 copy-start.5
  511.8 4.5 copy-start.11
  837.8 148.2 %copy-start.17 = (pred[128,128]{1,0:T(8,128)(4,1)S(1)}, pred[128,128]{1,0:T(8,128)(4,1)}, u32[]{:S(2)}) copy-start(pred[128,128]{1,0:T(8,128)(4,1)} %iota_compare_fusion.9) | copy-start | bytes 49156
  841.7 146.8 %copy-start.10 = (pred[768,768]{1,0:T(8,128)(4,1)S(1)}, pred[768,768]{1,0:T(8,128)(4,1)}, u32[]{:S(2)}) copy-start(pred[768,768]{1,0:T(8,128)(4,1)} %iota_compare_fusion.4) | copy-start | bytes 1769476
  1315.4 2.7 copy-start.3
  1345.6 2.7 copy-start.3
  (21 other events, 45.1 us)
Sparse Core Ops, SparseCore 0:
  332.9 57.0 all-reduce.7
where the time goes:
time: 1370 us; the launch traced here: 1360 us
  other arithmetic  816 us (60%)
  local copies, waits for them, and re-layouts  264 us (19%)
  matrix products  188 us (14%)
  waiting for transfers between devices  57.9 us (4%)
  between operations  14.9 us (1%)
    another operation x26, other arithmetic, local(): factor = jnp.linalg.cholesky(system)  490 us
    another operation x20, other arithmetic, local(): jax.scipy.linalg.cho_solve((chol_factor, True), vector)  246 us
    reshape x40, local copies, waits for them, and re-layouts, lag_sums(): flat.reshape(leading + (lag_count, width + 1))[..., 1:lag_count + 1]  81.1 us
    psum x1, waiting for transfers between devices, local(): corr, cross_whole = lax.psum((corr_part, cross_all), 'tm')  56.6 us
    another operation x10, matrix products, local(): factor = jnp.linalg.cholesky(system)  29.5 us
  transfers between devices with their start and end apart: 3, of which 3 were waited for; matrix products, arithmetic and copies ran while one was open for 0% of the time, Pallas kernels for 0%

commit v1 on v0

v1 whole, which is shorter than its diff:
```python
import math

import jax
import jax.numpy as jnp
from jax import lax
from jax.experimental import pallas as pl
from jax.experimental.pallas import tpu as pltpu
from jax.sharding import PartitionSpec as P

ACTIVE = 6817
DELAYS = 64
PER_RECV = 6


loading = 0.1
LANES = 128
MIB = 2**20
HIGHEST = lax.Precision.HIGHEST


def passed_along(array, axis, by):
    peers = lax.axis_size(axis)
    return lax.ppermute(array, axis, [(i, (i + by) % peers) for i in range(peers)])


def from_behind(block, axis, distance):
    devices = range(lax.axis_size(axis))
    route = [(i - distance, i) for i in devices if i - distance in devices]
    return lax.ppermute(block, axis, route)


def rotation_angle_grid(row_count, col_count, period):
    product = (
        jnp.arange(row_count, dtype=jnp.int32)[:, None]
        * jnp.arange(col_count, dtype=jnp.int32)[None, :]
    )
    phases = (product % period).astype(jnp.float32) * (2.0 * math.pi / period)
    return (jnp.cos(phases), jnp.sin(phases))


def complex_multiply_result(pattern, left_pair, right_pair):
    real_part = jnp.einsum(pattern, left_pair[0], right_pair[0], precision=HIGHEST) - jnp.einsum(
        pattern, left_pair[1], right_pair[1], precision=HIGHEST
    )
    imag_part = jnp.einsum(pattern, left_pair[0], right_pair[1], precision=HIGHEST) + jnp.einsum(
        pattern, left_pair[1], right_pair[0], precision=HIGHEST
    )
    return (real_part, imag_part)


def remodulate(symbols):
    emitter_number, length = symbols.shape
    column_entries = 128
    increment_spacing = length // column_entries
    inphase_amplitude = (2 * (symbols % 8) - 7).astype(jnp.float32) / math.sqrt(42.0)
    quadrature_amplitude = (2 * (symbols // 8) - 7).astype(jnp.float32) / math.sqrt(42.0)
    subcarrier = jnp.arange(length, dtype=jnp.int32) - length // 2
    occupied_tones = (jnp.abs(subcarrier) <= (ACTIVE - 1) // 2).astype(jnp.float32)
    tone_symbols = (
        (inphase_amplitude * occupied_tones).reshape(
            emitter_number, increment_spacing, column_entries
        ),
        (quadrature_amplitude * occupied_tones).reshape(
            emitter_number, increment_spacing, column_entries
        ),
    )
    partial_result = complex_multiply_result(
        "mb,nbd->nmd",
        rotation_angle_grid(increment_spacing, increment_spacing, increment_spacing),
        tone_symbols,
    )
    twiddle = rotation_angle_grid(increment_spacing, column_entries, length)
    partial_result = (
        partial_result[0] * twiddle[0] - partial_result[1] * twiddle[1],
        partial_result[0] * twiddle[1] + partial_result[1] * twiddle[0],
    )
    frequency_spectrum = complex_multiply_result(
        "pho,oj->phj",
        partial_result,
        rotation_angle_grid(column_entries, column_entries, column_entries),
    )
    alternate = (1 - 2 * (jnp.arange(length, dtype=jnp.int32) % 2)).astype(jnp.float32) / math.sqrt(
        ACTIVE
    )
    real_part = (
        jnp.swapaxes(frequency_spectrum[0], 1, 2).reshape(emitter_number, length) * alternate
    )
    imag_part = (
        jnp.swapaxes(frequency_spectrum[1], 1, 2).reshape(emitter_number, length) * alternate
    )
    return jnp.stack([real_part, imag_part], axis=1).astype(jnp.bfloat16)


def lanes_of(shape):
    return lax.broadcasted_iota(jnp.int32, shape, len(shape) - 1)


def rows_of(shape):
    return lax.broadcasted_iota(jnp.int32, shape, len(shape) - 2)


def half_turn(block):
    return pltpu.roll(block, LANES // 2, 1)


def signal_matrix(re, im):
    low = lanes_of(re.shape) < LANES // 2
    turned_re, turned_im = half_turn(re), half_turn(im)
    return jnp.concatenate(
        [
            jnp.where(low, re, turned_im),
            jnp.where(low, turned_re, im),
            jnp.where(low, im, -turned_re),
            jnp.where(low, turned_im, -re),
        ],
        axis=0,
    ).astype(jnp.bfloat16)


def fold_lags(product):
    half = LANES // 2
    shape = (half, LANES)
    earlier = lanes_of(shape) % half < rows_of(shape)
    total = jnp.where(earlier, half_turn(product[:half]), product[half:])
    rows = half // 2
    while rows >= 8:
        total = total[:rows] + pltpu.roll(total[rows:], LANES - rows, 1)
        rows //= 2
    for step in (4, 2, 1):
        total = total + pltpu.roll(pltpu.roll(total, LANES - step, 1), 8 - step, 0)
    return total[:1]


def front_kernel(
    slots, delays, gains, x_ref, xp_ref, echo_ref, recv_ref, corr_ref, cross_ref, fq_ref, ft_ref
):
    window, _, rows, _ = x_ref.shape
    recv_count = echo_ref.shape[1]
    lane = lanes_of((rows, LANES))
    low = lane < LANES // 2

    def frame(i, carry):
        parts = []
        for c in range(2):
            x = x_ref[i, c]
            parts += [half_turn(jnp.where(low, x, xp_ref[i, c])), x]
        whole = jnp.concatenate(parts, axis=0)
        fq_ref[i] = whole.astype(jnp.bfloat16)
        ft_ref[i] = whole.T.astype(jnp.bfloat16)
        return carry

    lax.fori_loop(0, window, frame, 0)

    def pairs(j, carry):
        matrix = signal_matrix(x_ref[j, 0], x_ref[j, 1])
        for i in range(window):
            product = jnp.dot(ft_ref[i], matrix, preferred_element_type=jnp.float32)
            corr_ref[j, i : i + 1, :] = fold_lags(product)
        return carry

    lax.fori_loop(0, window, pairs, 0)

    def receiver(r, carry):
        re = jnp.zeros((rows, LANES), jnp.float32)
        im = jnp.zeros((rows, LANES), jnp.float32)
        for k in range(PER_RECV):
            s = slots[r, k]
            d = delays[r, k]
            g_re = gains[0, r, k]
            g_im = gains[1, r, k]
            wrapped = lane >= LANES - d
            y_re = pltpu.roll(jnp.where(wrapped, xp_ref[s, 0], x_ref[s, 0]), d, 1)
            y_im = pltpu.roll(jnp.where(wrapped, xp_ref[s, 1], x_ref[s, 1]), d, 1)
            re = re + (g_re * y_re - g_im * y_im)
            im = im + (g_re * y_im + g_im * y_re)
        re = (echo_ref[0, r].astype(jnp.float32) + re).astype(jnp.bfloat16)
        im = (echo_ref[1, r].astype(jnp.float32) + im).astype(jnp.bfloat16)
        recv_ref[0, r] = re
        recv_ref[1, r] = im
        matrix = signal_matrix(re.astype(jnp.float32), im.astype(jnp.float32))
        for k in range(PER_RECV):
            product = jnp.dot(ft_ref[slots[r, k]], matrix, preferred_element_type=jnp.float32)
            cross_ref[r, k : k + 1, :] = fold_lags(product)
        return carry

    lax.fori_loop(0, recv_count, receiver, 0)


def back_kernel(slots, taps_ref, fq_ref, recv_ref, out_ref):
    recv_count, rows = recv_ref.shape[1:3]
    half = LANES // 2
    shape = (LANES, LANES)
    place = lanes_of(shape) % half
    row = rows_of(shape)
    valid = ((row < half) & (place < row)) | ((row >= half) & (place >= row - half))
    low = lanes_of((LANES, LANES)) < half
    low_half = lanes_of((rows, LANES)) < half

    def receiver(r, carry):
        total = jnp.zeros((4 * rows, LANES), jnp.float32)
        for k in range(PER_RECV):
            base = jnp.broadcast_to(taps_ref[r, k : k + 1, :], shape)
            band = pltpu.roll(base, half, 1, stride=1, stride_axis=0)
            band = jnp.where(valid, band, 0.0).astype(jnp.bfloat16)
            total = total + jnp.dot(
                fq_ref[slots[r, k]], band, preferred_element_type=jnp.float32
            )
        turned = half_turn(total[2 * rows :])
        both = total[: 2 * rows] + jnp.where(low, -turned, turned)
        first, second = both[:rows], both[rows:]
        re = jnp.where(low_half, first, half_turn(second))
        im = jnp.where(low_half, half_turn(first), second)
        out_ref[0, r] = (recv_ref[0, r].astype(jnp.float32) - re).astype(jnp.bfloat16)
        out_ref[1, r] = (recv_ref[1, r].astype(jnp.float32) - im).astype(jnp.bfloat16)
        return carry

    lax.fori_loop(0, recv_count, receiver, 0)


def times_i(block):
    pieces = []
    for start in range(0, block.shape[1], LANES):
        turned = half_turn(block[:, start : start + LANES])
        pieces.append(jnp.where(lanes_of(turned.shape) < LANES // 2, -turned, turned))
    return jnp.concatenate(pieces, axis=1)


def complex_dot(left, right):
    return jnp.dot(left, right, precision=HIGHEST, preferred_element_type=jnp.float32)


def as_real(block):
    return jnp.concatenate([block, times_i(block)], axis=0)


def invert(blocks):
    size = blocks[0].shape[0]
    lane = lanes_of(blocks[0].shape)
    row_id = rows_of(blocks[0].shape)
    lane_row = lanes_of((1, LANES))
    blocks = list(blocks)
    for j in range(size):
        for s, a in enumerate(blocks):
            pivot = 1.0 / a[j : j + 1, j : j + 1]
            row = jnp.where(lane_row == j, 1.0, jnp.where(lane_row == size + j, 0.0, a[j : j + 1]))
            row = row * pivot
            turned = half_turn(row)
            row_i = jnp.where(lane_row < size, -turned, turned)
            rest = jnp.where((lane == j) | (lane == size + j), 0.0, a)
            rest = rest - a[:, j : j + 1] * row - a[:, size + j : size + j + 1] * row_i
            blocks[s] = jnp.where(row_id == j, row, rest)
    return blocks


def solve_kernel(slots, vr_ref, vi_ref, rhs_ref, out_ref, a_ref, d_ref):
    share = rhs_ref.shape[0]
    size = DELAYS
    window = math.isqrt(vr_ref.shape[0])
    shape = (size, LANES)
    lane, row_id = lanes_of(shape), rows_of(shape)
    low = lane < size
    unit = jnp.where(lane == row_id, jnp.float32(loading), 0.0)
    end = PER_RECV * LANES

    def build(index, carry):
        s, k = index // PER_RECV, index % PER_RECV
        start = pl.multiple_of(k * size, size)
        first = slots[s, k]
        for l in range(PER_RECV):
            at = first * window + slots[s, l]
            re = jnp.broadcast_to(vr_ref[at], shape)
            im = jnp.broadcast_to(vi_ref[at], shape)
            block = jnp.where(
                low,
                pltpu.roll(re, 0, 1, stride=1, stride_axis=0),
                pltpu.roll(im, size, 1, stride=1, stride_axis=0),
            )
            block = block + jnp.where(k == l, unit, 0.0)
            a_ref[s, pl.ds(start, size), l * LANES : (l + 1) * LANES] = block
        side = rhs_ref[s, pl.ds(start, size), :]
        a_ref[s, pl.ds(start, size), end : end + LANES] = jnp.where(
            lane == 0, side[:, 0:1], jnp.where(lane == size, side[:, 1:2], 0.0)
        )
        return carry

    lax.fori_loop(0, share * PER_RECV, build, 0)

    def eliminate(p, carry):
        at_row = pl.multiple_of(p * size, size)
        at_col = pl.multiple_of(p * LANES, LANES)
        blocks = [a_ref[s, pl.ds(at_row, size), pl.ds(at_col, LANES)] for s in range(share)]
        for s, block in enumerate(invert(blocks)):
            d_ref[s] = block
        for step in range(PER_RECV):

            @pl.when(p == step)
            def _():
                top, left = step * size, (step + 1) * LANES
                for s in range(share):
                    right = a_ref[s, top : top + size, left:]
                    scaled = complex_dot(d_ref[s], as_real(right))
                    a_ref[s, top : top + size, left:] = scaled
                    if step < PER_RECV - 1:
                        below = a_ref[s, top + size :, left - LANES : left]
                        a_ref[s, top + size :, left:] -= complex_dot(below, as_real(scaled))

        return carry

    lax.fori_loop(0, PER_RECV, eliminate, 0)
    for s in range(share):
        known = None
        for p in reversed(range(PER_RECV)):
            top, left = p * size, (p + 1) * LANES
            found = a_ref[s, top : top + size, end : end + LANES]
            if known is not None:
                found = found - complex_dot(a_ref[s, top : top + size, left:end], known)
            out_ref[s, top : top + size, :] = found
            found = as_real(found)
            known = found if known is None else jnp.concatenate([found, known], axis=0)


def kernel_call(body, outs, scalars, arrays, scratch=()):
    spec_smem = pl.BlockSpec(memory_space=pltpu.SMEM)
    spec_vmem = pl.BlockSpec(memory_space=pltpu.VMEM)
    return pl.pallas_call(
        body,
        out_shape=outs,
        in_specs=[spec_smem] * len(scalars) + [spec_vmem] * len(arrays),
        out_specs=jax.tree.map(lambda _: spec_vmem, outs),
        scratch_shapes=list(scratch),
        compiler_params=pltpu.CompilerParams(vmem_limit_bytes=48 * MIB),
    )(*scalars, *arrays)


def local(symbols, incidence, delays, gains, echoes):
    local_refs = remodulate(symbols)
    owned = local_refs.shape[0]
    length = local_refs.shape[2]
    rows = length // LANES
    taps_count = PER_RECV * DELAYS
    chan_count = lax.axis_size("chan")
    chan_index = lax.axis_index("chan")
    tm_count = lax.axis_size("tm")
    tm_index = lax.axis_index("tm")
    window_count = 2 * owned
    recv_count = echoes.shape[1]
    following = passed_along(local_refs, "chan", -1)
    window = jnp.concatenate([local_refs, following], axis=0)
    previous = from_behind(window[:, :, length - DELAYS :], "tm", 1)
    previous = jnp.pad(previous, ((0, 0), (0, 0), (LANES - DELAYS, 0)))[:, :, None, :]
    x = window.reshape(window_count, 2, rows, LANES)
    xp = jnp.concatenate([previous, x[:, :, :-1]], axis=2).astype(jnp.float32)
    x = x.astype(jnp.float32)
    owner_chan = incidence // owned
    slot = (owner_chan - chan_index) % chan_count * owned + incidence % owned
    received, corr_part, cross_part, frames = kernel_call(
        front_kernel,
        (
            jax.ShapeDtypeStruct((2, recv_count, rows, LANES), jnp.bfloat16),
            jax.ShapeDtypeStruct((window_count, window_count, LANES), jnp.float32),
            jax.ShapeDtypeStruct((recv_count, PER_RECV, LANES), jnp.float32),
            jax.ShapeDtypeStruct((window_count, 4 * rows, LANES), jnp.bfloat16),
        ),
        (slot, delays, gains),
        (x, xp, echoes.reshape(2, recv_count, rows, LANES)),
        (pltpu.VMEM((window_count, LANES, 4 * rows), jnp.bfloat16),),
    )
    share = recv_count // tm_count
    scale = 1.0 / (length * tm_count)
    corr, cross_whole = lax.psum((corr_part, cross_part), "tm")
    corr = corr * scale
    cross = lax.dynamic_slice_in_dim(cross_whole, tm_index * share, share, 0) * scale
    mine = lax.dynamic_slice_in_dim(slot, tm_index * share, share, 0)
    swapped = jnp.swapaxes(corr, 0, 1)
    gap = jnp.zeros(corr.shape[:2] + (1,), jnp.float32)

    def diagonals(ahead, behind, sign):
        line = jnp.concatenate(
            [ahead[..., :1], sign * behind[..., 1:], gap, jnp.flip(ahead[..., 1:], axis=-1)], axis=-1
        )
        return line.reshape(window_count * window_count, 1, LANES)

    vr = diagonals(swapped[..., :DELAYS], corr[..., :DELAYS], 1.0)
    vi = diagonals(swapped[..., DELAYS:], corr[..., DELAYS:], -1.0)
    rhs = cross.reshape(share, PER_RECV, 2, DELAYS).swapaxes(2, 3).reshape(share, taps_count, 2)
    solved = kernel_call(
        solve_kernel,
        jax.ShapeDtypeStruct((share, taps_count, LANES), jnp.float32),
        (mine,),
        (vr, vi, rhs),
        (
            pltpu.VMEM((share, taps_count, (PER_RECV + 1) * LANES), jnp.float32),
            pltpu.VMEM((share, DELAYS, LANES), jnp.float32),
        ),
    )
    local_weights = jnp.stack([solved[:, :, 0], solved[:, :, DELAYS]])
    weights = lax.all_gather(local_weights, "tm", axis=1, tiled=True)
    taps = weights.astype(jnp.bfloat16).astype(jnp.float32)
    taps = taps.reshape(2, recv_count, PER_RECV, DELAYS).transpose(1, 2, 0, 3)
    taps = taps.reshape(recv_count, PER_RECV, LANES)
    cancelled = kernel_call(
        back_kernel,
        jax.ShapeDtypeStruct((2, recv_count, rows, LANES), jnp.bfloat16),
        (slot,),
        (taps, frames, received),
    )
    return (cancelled.reshape(2, recv_count, length), weights)


def solution(mesh):
    in_specs = (
        P("chan", "tm"),
        P("chan", None),
        P("chan", None),
        P(None, "chan", None),
        P(None, "chan", "tm"),
    )
    out_specs = (P(None, "chan", "tm"), P(None, "chan", None))
    return jax.shard_map(local, mesh=mesh, in_specs=in_specs, out_specs=out_specs, check_vma=False)
```

time: 1370 us -> 287 us (0.21)
  other arithmetic: 816 us -> 5.48 us
  local copies, waits for them, and re-layouts: 264 us -> 6.62 us
  matrix products: 188 us -> 4.59 us
  Pallas kernels: 0 us -> 177 us
    another operation x52 -> x2, other arithmetic: 737 us -> 0.05 us  [the longest x26 490 us: local(): factor = jnp.linalg.cholesky(system)]
    pallas_call x0 -> x3, Pallas kernels: none -> 177 us  [kernel_call(): pl.pallas_call(body, out_shape=outs, in_specs=[spec_smem] * len(scalars)...]
    reshape x86 -> x6, local copies, waits for them, and re-layouts: 122 us -> 1.78 us  [the longest x1 1.27 us: local(): return (cancelled.reshape(2, recv_count, length), weights)]
    dot_general x78 -> x0, matrix products: 117 us -> none  [the longest x12 21 us: banded_apply(): jnp.einsum('bkqv,bkvp->bqp', looked[:, :, 1], banded[1], preferred_elemen...]
    another operation x32 -> x0, matrix products: 53.4 us -> none  [the longest x10 29.5 us: local(): factor = jnp.linalg.cholesky(system)]
    another operation x34 -> x1, local copies, waits for them, and re-layouts: 30.2 us -> 0.01 us  [local(): local_weights = jnp.stack([solved[:, :, 0], solved[:, :, DELAYS]])]
    reduce_sum x40 -> x0, other arithmetic: 22 us -> none  [lag_sums(): return jnp.flip(jnp.sum(skewed, axis=-2), axis=-1)]
    gather x8 -> x0, local copies, waits for them, and re-layouts: 21.7 us -> none  [the longest x4 10.8 us: second_pass(): jnp.take(frames, slots, axis=0)]
where the time goes in v1:
time: 287 us; the launch traced here: 286 us
  Pallas kernels  177 us (62%)
  waiting for transfers between devices  63.2 us (22%)
  between operations  14.3 us (5%)
  blocking collectives  8.52 us (3%)
  local copies, waits for them, and re-layouts  6.62 us (2%)
  starting transfers between devices  6.45 us (2%)
  other arithmetic  5.48 us (2%)
  matrix products  4.59 us (2%)
    pallas_call x3, Pallas kernels, kernel_call(): pl.pallas_call(body, out_shape=outs, in_specs=[spec_smem] * len(scalars)...  177 us
    psum x1, waiting for transfers between devices, local(): corr, cross_whole = lax.psum((corr_part, cross_part), 'tm')  58.5 us
    all_gather x1, blocking collectives, local(): weights = lax.all_gather(local_weights, 'tm', axis=1, tiled=True)  8.52 us
  transfers between devices with their start and end apart: 3, of which 3 were waited for; matrix products, arithmetic and copies ran while one was open for 0% of the time, Pallas kernels for 0%

profile of v1, /device:TPU:0, one launch (start us, length us, event | category | flops | bytes accessed | tf_op | source)
XLA Modules:
  0.0 286.4 jit_solution(4766698672794203690)
XLA Ops:
  7.4 1.2 fusion.8
  9.7 0.5 fusion.3
  10.2 0.5 fusion.2
  10.8 0.6 fusion.25
  11.4 0.6 fusion.29
  12.1 0.6 fusion
  13.1 0.6 fusion.1
  14.2 5.1 %collective-permute-start = (bf16[8,2,8192]{2,0,1:T(8,128)(2,1)S(1)}, bf16[8,2,8192]{2,0,1:T(8,128)(2,1)S(1)}, u32[]{:S(2)}, u32[]{:S(2)}) collective-permute-start(bf16[8,2,8192]{2,0,1:T(8,128)(2,1)S(1)} %pad_maximum_fusion.1), channel_id=1, source_target_pairs={{0,24},{8,0},{16,8},{24,16},{1,25},{9,1},{17,9},{25,17},{2,26},{10... | collective-permute-start | bytes 786440 | tf_op jit(solution)/shard_map/ppermute | solution.py:23
  20.2 0.6 copy-done.3
  20.9 3.9 %collective-permute-done = bf16[8,2,8192]{2,0,1:T(8,128)(2,1)S(1)} collective-permute-done((bf16[8,2,8192]{2,0,1:T(8,128)(2,1)S(1)}, bf16[8,2,8192]{2,0,1:T(8,128)(2,1)S(1)}, u32[]{:S(2)}, u32[]{:S(2)}) %collective-permute-start) | collective-permute-done | bytes 262176 | tf_op jit(solution)/shard_map/ppermute | solution.py:23
  25.1 1.3 collective-permute-start.1
  26.5 0.7 collective-permute-done.1
  27.5 51.2 %shard_map.68 = (bf16[2,32,64,128]{3,2,1,0:T(8,128)(2,1)S(1)}, f32[16,16,128]{2,1,0:T(8,128)}, f32[32,6,128]{2,1,0:T(8,128)}, bf16[16,256,128]{2,1,0:T(8,128)(2,1)S(1)}) custom-call(s32[32,6]{1,0:T(8,128)S(1)} %fusion.67.slots, s32[32,6]{1,0:T(8,128)S(1)} %copy.73.delays, f32[2,32,6]{2,1,0:T(8,128)S(1)} %copy.74.gains, ...), custom_call_target="tpu_custom_call" | custom-call | tf_op jit(solution)/shard_map/pallas_call | solution.py:325
  78.8 58.5 %all-reduce.4.cloned.1.call-done = (f32[16,16,128]{2,1,0:T(8,128)}, f32[32,6,128]{2,1,0:T(8,128)}) async-done(((f32[16,16,128]{2,1,0:T(8,128)}, f32[32,6,128]{2,1,0:T(8,128)}), (f32[16,16,128]{2,1,0:T(8,128)}, f32[32,6,128]{2,1,0:T(8,128)})) %all-reduce.4.cloned.1.call-update) | async-done | bytes 229392 | tf_op jit(solution)/shard_map/psum | solution.py:370
  137.4 0.9 broadcast_multiply_fusion
  138.6 0.8 slice_multiply_fusion
  139.6 0.7 dynamic-slice_multiply_fusion
  140.7 1.2 pad_maximum_fusion.3
  141.9 110.1 %shard_map.69 = f32[4,384,128]{2,1,0:T(8,128)S(1)} custom-call(s32[4,6]{1,0:T(4,128)S(1)} %constant_dynamic-slice_fusion.slots, f32[256,1,128]{2,1,0:T(1,128)S(1)} %bitcast.62, f32[256,1,128]{2,1,0:T(1,128)S(1)} %bitcast.61, f32[4,384,2]{2,1,0:T(8,128)S(1)} %bitcast.60), custom_call_target="tpu_custom_call" | custom-call | tf_op jit(solution)/shard_map/pallas_call | solution.py:325
  252.0 0.7 slice_reduce_fusion.1
  252.8 8.5 %all_gather.3 = f32[2,32,384]{2,0,1:T(2,128)S(1)} all-gather(f32[2,4,384]{2,0,1:T(2,128)S(1)} %copy.78), channel_id=1, replica_groups=mesh['chan'=4,'tm'=8] {'tm'}, dimensions={1}, use_global_device_ids=true | all-gather | bytes 110592 | tf_op jit(solution)/shard_map/all_gather | solution.py:397
  261.3 0.6 copy.82
  262.4 15.9 %shard_map.70 = bf16[2,32,64,128]{3,2,1,0:T(8,128)(2,1)S(1)} custom-call(s32[32,6]{1,0:T(8,128)S(1)} %fusion.67.slots, f32[32,6,128]{2,1,0:T(8,128)S(1)} %reshape.182.taps_ref, bf16[16,256,128]{2,1,0:T(8,128)(2,1)S(1)} %get-tuple-element.8.fq_ref, bf16[2,32,64,128]{3,2,1,0:T(8,128)(2,1)S(1)} %get-tuple-element.9.recv_ref), custom_call_target="tpu_custom_call" | custom-call | tf_op jit(solution)/shard_map/pallas_call | solution.py:325
  278.3 1.3 reshape.171
  (49 shorter events, 5.1 us)
Async XLA Ops:
  7.2 130.2 %all-reduce.4.cloned.1.call-start = ((), (), s32[]{:S(2)}) async-start(), calls=%async_computation | async-start | bytes 524288 | tf_op jit(solution)/shard_map/psum | solution.py:370
  13.9 5.5 %copy-start = (bf16[2,32,8192]{2,1,0:T(8,128)(2,1)S(1)}, bf16[2,32,8192]{2,1,0:T(8,128)(2,1)}, u32[]{:S(2)}) copy-start(bf16[2,32,8192]{2,1,0:T(8,128)(2,1)} %param.9) | copy-start | bytes 3145732
  14.2 5.1 %copy-start.2 = (s32[32,6]{0,1:T(8,128)S(1)}, s32[32,6]{0,1:T(8,128)}, u32[]{:S(2)}) copy-start(s32[32,6]{0,1:T(8,128)} %param.6) | copy-start | bytes 2308
  14.2 10.7 %collective-permute-start = (bf16[8,2,8192]{2,0,1:T(8,128)(2,1)S(1)}, bf16[8,2,8192]{2,0,1:T(8,128)(2,1)S(1)}, u32[]{:S(2)}, u32[]{:S(2)}) collective-permute-start(bf16[8,2,8192]{2,0,1:T(8,128)(2,1)S(1)} %pad_maximum_fusion.1), channel_id=1, source_target_pairs={{0,24},{8,0},{16,8},{24,16},{1,25},{9,1},{17,9},{25,17},{2,26},{10... | collective-permute-start | bytes 786440 | tf_op jit(solution)/shard_map/ppermute | solution.py:23
  19.4 0.7 copy-start.1
  20.1 0.7 copy-start.3
  25.1 2.1 collective-permute-start.1
Sparse Core Ops, SparseCore 0:
  78.8 58.4 all-reduce.3

commit v2 on v1

--- a/solution.py
+++ b/solution.py
@@ -101,6 +101,17 @@
 
 def half_turn(block):
     return pltpu.roll(block, LANES // 2, 1)
+
+
+def several(count, together, body):
+    together = math.gcd(count, together)
+
+    def step(i, carry):
+        for t in range(together):
+            carry = body(i * together + t, carry)
+        return carry
+
+    lax.fori_loop(0, count // together, step, 0)
 
 
 def signal_matrix(re, im):
@@ -183,7 +194,7 @@
             cross_ref[r, k : k + 1, :] = fold_lags(product)
         return carry
 
-    lax.fori_loop(0, recv_count, receiver, 0)
+    several(recv_count, 2, receiver)
 
 
 def back_kernel(slots, taps_ref, fq_ref, recv_ref, out_ref):
@@ -214,7 +225,7 @@
         out_ref[1, r] = (recv_ref[1, r].astype(jnp.float32) - im).astype(jnp.bfloat16)
         return carry
 
-    lax.fori_loop(0, recv_count, receiver, 0)
+    several(recv_count, 4, receiver)
 
 
 def times_i(block):
@@ -235,20 +246,37 @@
 
 def invert(blocks):
     size = blocks[0].shape[0]
-    lane = lanes_of(blocks[0].shape)
-    row_id = rows_of(blocks[0].shape)
-    lane_row = lanes_of((1, LANES))
+    panel = 8
+    shape = (panel, LANES)
+    lane, row_id = lanes_of(shape), rows_of(shape)
+    group = lanes_of(blocks[0].shape) % size // panel
     blocks = list(blocks)
-    for j in range(size):
-        for s, a in enumerate(blocks):
-            pivot = 1.0 / a[j : j + 1, j : j + 1]
-            row = jnp.where(lane_row == j, 1.0, jnp.where(lane_row == size + j, 0.0, a[j : j + 1]))
-            row = row * pivot
-            turned = half_turn(row)
-            row_i = jnp.where(lane_row < size, -turned, turned)
-            rest = jnp.where((lane == j) | (lane == size + j), 0.0, a)
-            rest = rest - a[:, j : j + 1] * row - a[:, size + j : size + j + 1] * row_i
-            blocks[s] = jnp.where(row_id == j, row, rest)
+    for start in range(0, size, panel):
+        panels = [a[start : start + panel] for a in blocks]
+        for t in range(panel):
+            j = start + t
+            for s, rows in enumerate(panels):
+                col_re = jnp.broadcast_to(rows[:, j : j + 1], shape)
+                col_im = jnp.broadcast_to(rows[:, size + j : size + j + 1], shape)
+                pivot = 1.0 / col_re[t : t + 1]
+                rest = jnp.where((lane == j) | (lane == size + j), 0.0, rows)
+                row = jnp.where(lane[:1] == j, 1.0, rest[t : t + 1])
+                turned = half_turn(row)
+                row_i = jnp.where(lane[:1] < size, -turned, turned) * pivot
+                row = row * pivot
+                rest = rest - col_re * row - col_im * row_i
+                panels[s] = jnp.where(row_id == t, row, rest)
+        chosen = group == start // panel
+        for s, (a, rows) in enumerate(zip(blocks, panels)):
+            above = [jnp.zeros((start, LANES), jnp.float32)] if start > 0 else []
+            left = size - panel - start
+            below = [jnp.zeros((left, LANES), jnp.float32)] if left > 0 else []
+            pieces = above + [rows] + below + above + [times_i(rows)] + below
+            change = complex_dot(jnp.where(chosen, a, 0.0), jnp.concatenate(pieces, axis=0))
+            rest = jnp.where(chosen, 0.0, a) - change
+            above = [rest[:start]] if start > 0 else []
+            below = [rest[start + panel :]] if left > 0 else []
+            blocks[s] = jnp.concatenate(above + [rows] + below, axis=0)
     return blocks
 
 
@@ -319,7 +347,7 @@
             known = found if known is None else jnp.concatenate([found, known], axis=0)
 
 
-def kernel_call(body, outs, scalars, arrays, scratch=()):
+def kernel_call(body, outs, scalars, arrays, scratch=(), **params):
     spec_smem = pl.BlockSpec(memory_space=pltpu.SMEM)
     spec_vmem = pl.BlockSpec(memory_space=pltpu.VMEM)
     return pl.pallas_call(
@@ -328,8 +356,122 @@
         in_specs=[spec_smem] * len(scalars) + [spec_vmem] * len(arrays),
         out_specs=jax.tree.map(lambda _: spec_vmem, outs),
         scratch_shapes=list(scratch),
-        compiler_params=pltpu.CompilerParams(vmem_limit_bytes=48 * MIB),
+        compiler_params=pltpu.CompilerParams(vmem_limit_bytes=48 * MIB, **params),
     )(*scalars, *arrays)
+
+
+def peer(offset):
+    count = lax.axis_size("tm")
+    return lax.rem(lax.axis_index("tm") + offset, count)
+
+
+def greet():
+    count = lax.axis_size("tm")
+    barrier = pltpu.get_barrier_semaphore()
+    for offset in range(1, count):
+        pl.semaphore_signal(
+            barrier,
+            inc=1,
+            device_id={"tm": peer(offset)},
+            device_id_type=pl.DeviceIdType.MESH,
+        )
+    pl.semaphore_wait(barrier, count - 1)
+
+
+def push(source, target, sends, arrivals, offset):
+    copy = pltpu.make_async_remote_copy(
+        src_ref=source,
+        dst_ref=target,
+        send_sem=sends.at[offset],
+        recv_sem=arrivals.at[offset],
+        device_id={"tm": peer(offset)},
+        device_id_type=pl.DeviceIdType.MESH,
+    )
+    copy.start()
+    return copy
+
+
+def sum_kernel(
+    corr_ref, cross_ref, corr_out, cross_out, corr_in, cross_in, s0, r0, s1, r1, s2, r2
+):
+    count, rows = corr_in.shape[:2]
+    share = cross_in.shape[1]
+    me = lax.axis_index("tm")
+    own_rows = pl.ds(pl.multiple_of(me * rows, rows), rows)
+    own_share = pl.ds(me * share, share)
+    greet()
+    copies = []
+    for offset in range(1, count):
+        to = peer(offset)
+        their_rows = pl.ds(pl.multiple_of(to * rows, rows), rows)
+        their_share = pl.ds(to * share, share)
+        copies.append(push(corr_ref.at[their_rows], corr_in.at[offset], s0, r0, offset))
+        copies.append(push(cross_ref.at[their_share], cross_in.at[offset], s1, r1, offset))
+    for copy in copies[::2]:
+        copy.wait()
+    total = corr_ref[own_rows, :]
+    for offset in range(1, count):
+        total = total + corr_in[offset]
+    corr_out[own_rows, :] = total
+    spread = [
+        push(corr_out.at[own_rows], corr_out.at[own_rows], s2, r2, offset)
+        for offset in range(1, count)
+    ]
+    for copy in copies[1::2]:
+        copy.wait()
+    total = cross_ref[own_share]
+    for offset in range(1, count):
+        total = total + cross_in[offset]
+    cross_out[...] = total
+    for copy in spread:
+        copy.wait()
+
+
+def gather_kernel(in_ref, out_ref, sends, arrivals):
+    count = out_ref.shape[0]
+    me = lax.axis_index("tm")
+    greet()
+    copies = [push(in_ref, out_ref.at[me], sends, arrivals, o) for o in range(1, count)]
+    out_ref[me] = in_ref[...]
+    for copy in copies:
+        copy.wait()
+
+
+def window_sums(corr_part, cross_part):
+    count = lax.axis_size("tm")
+    shares = (cross_part.shape[0] // count,) + cross_part.shape[1:]
+    flat = corr_part.reshape(-1, LANES)
+    rows = flat.shape[0] // count
+    corr, cross = kernel_call(
+        sum_kernel,
+        (
+            jax.ShapeDtypeStruct(flat.shape, jnp.float32),
+            jax.ShapeDtypeStruct(shares, jnp.float32),
+        ),
+        (),
+        (flat, cross_part),
+        (
+            pltpu.VMEM((count, rows, LANES), jnp.float32),
+            pltpu.VMEM((count,) + shares, jnp.float32),
+        )
+        + (pltpu.SemaphoreType.DMA((count,)),) * 6,
+        collective_id=0,
+        has_side_effects=True,
+    )
+    return corr.reshape(corr_part.shape), cross
+
+
+def gathered_weights(solved):
+    count = lax.axis_size("tm")
+    return kernel_call(
+        gather_kernel,
+        jax.ShapeDtypeStruct((count,) + solved.shape, jnp.float32),
+        (),
+        (solved,),
+        (pltpu.SemaphoreType.DMA((count,)),) * 2,
+        collective_id=1,
+        has_side_effects=True,
+    )
 
 
 def local(symbols, incidence, delays, gains, echoes):
@@ -367,9 +509,9 @@
     )
     share = recv_count // tm_count
     scale = 1.0 / (length * tm_count)
-    corr, cross_whole = lax.psum((corr_part, cross_part), "tm")
+    corr, cross = window_sums(corr_part, cross_part)
     corr = corr * scale
-    cross = lax.dynamic_slice_in_dim(cross_whole, tm_index * share, share, 0) * scale
+    cross = cross * scale
     mine = lax.dynamic_slice_in_dim(slot, tm_index * share, share, 0)
     swapped = jnp.swapaxes(corr, 0, 1)
     gap = jnp.zeros(corr.shape[:2] + (1,), jnp.float32)
@@ -393,10 +535,12 @@
             pltpu.VMEM((share, DELAYS, LANES), jnp.float32),
         ),
     )
-    local_weights = jnp.stack([solved[:, :, 0], solved[:, :, DELAYS]])
-    weights = lax.all_gather(local_weights, "tm", axis=1, tiled=True)
-    taps = weights.astype(jnp.bfloat16).astype(jnp.float32)
-    taps = taps.reshape(2, recv_count, PER_RECV, DELAYS).transpose(1, 2, 0, 3)
+    local_weights = jnp.stack([solved[:, :, 0], solved[:, :, DELAYS]], axis=1)
+    gathered = gathered_weights(local_weights.reshape(share * 2, taps_count))
+    gathered = gathered.reshape(recv_count, 2, taps_count)
+    weights = jnp.swapaxes(gathered, 0, 1)
+    taps = gathered.astype(jnp.bfloat16).astype(jnp.float32)
+    taps = taps.reshape(recv_count, 2, PER_RECV, DELAYS).swapaxes(1, 2)
     taps = taps.reshape(recv_count, PER_RECV, LANES)
     cancelled = kernel_call(
         back_kernel,

time: 287 us -> 163 us (0.57)
  waiting for transfers between devices: 63.2 us -> 4.59 us
  Pallas kernels: 177 us -> 135 us
  between operations: 14.3 us -> 0.98 us
  blocking collectives: 8.52 us -> 0 us
    psum x1 -> x0, waiting for transfers between devices: 58.5 us -> none  [local(): corr, cross_whole = lax.psum((corr_part, cross_part), 'tm')]
    pallas_call x3 -> x5, Pallas kernels: 177 us -> 135 us  [kernel_call(): pl.pallas_call(body, out_shape=outs, in_specs=[spec_smem] * len(scalars)...]
    all_gather x1 -> x0, blocking collectives: 8.52 us -> none  [local(): weights = lax.all_gather(local_weights, 'tm', axis=1, tiled=True)]
  transfers between devices with their start and end apart: 3 -> 2, of which waited for: 3 -> 2; matrix products, arithmetic and copies ran while one was open for 0% -> 0% of each run, Pallas kernels for 0% -> 0%
where the time goes in v2:
time: 163 us; the launch traced here: 162 us
  Pallas kernels  135 us (83%)
  local copies, waits for them, and re-layouts  6.63 us (4%)
  starting transfers between devices  6.38 us (4%)
  matrix products  4.61 us (3%)
  waiting for transfers between devices  4.59 us (3%)
  other arithmetic  3.83 us (2%)
    pallas_call x5, Pallas kernels, kernel_call(): pl.pallas_call(body, out_shape=outs, in_specs=[spec_smem] * len(scalars)...  135 us
    ppermute x1, starting transfers between devices, passed_along(): lax.ppermute(array, axis, [(i, (i + by) % peers) for i in range(peers)])  5.09 us
    ppermute x1, waiting for transfers between devices, passed_along(): lax.ppermute(array, axis, [(i, (i + by) % peers) for i in range(peers)])  3.89 us
  transfers between devices with their start and end apart: 2, of which 2 were waited for; matrix products, arithmetic and copies ran while one was open for 0% of the time, Pallas kernels for 0%

profile of v2, /device:TPU:0, one launch (start us, length us, event | category | flops | bytes accessed | tf_op | source)
XLA Modules:
  0.0 162.3 jit_solution(9118489972793581850)
XLA Ops:
  0.8 1.2 fusion.8
  2.0 0.5 fusion.19
  2.6 0.5 fusion.15
  3.1 0.5 fusion.3
  3.7 0.5 fusion.2
  4.2 0.6 fusion.25
  4.8 0.6 fusion.29
  5.5 0.6 fusion
  6.5 0.6 fusion.1
  7.6 5.1 %collective-permute-start = (bf16[8,2,8192]{2,0,1:T(8,128)(2,1)S(1)}, bf16[8,2,8192]{2,0,1:T(8,128)(2,1)S(1)}, u32[]{:S(2)}, u32[]{:S(2)}) collective-permute-start(bf16[8,2,8192]{2,0,1:T(8,128)(2,1)S(1)} %pad_maximum_fusion.1), channel_id=1, source_target_pairs={{0,24},{8,0},{16,8},{24,16},{1,25},{9,1},{17,9},{25,17},{2,26},{10... | collective-permute-start | bytes 786440 | tf_op jit(solution)/shard_map/ppermute | solution.py:23
  13.6 0.6 copy-done.3
  14.4 3.9 %collective-permute-done = bf16[8,2,8192]{2,0,1:T(8,128)(2,1)S(1)} collective-permute-done((bf16[8,2,8192]{2,0,1:T(8,128)(2,1)S(1)}, bf16[8,2,8192]{2,0,1:T(8,128)(2,1)S(1)}, u32[]{:S(2)}, u32[]{:S(2)}) %collective-permute-start) | collective-permute-done | bytes 262176 | tf_op jit(solution)/shard_map/ppermute | solution.py:23
  18.5 1.3 collective-permute-start.1
  19.9 0.7 collective-permute-done.1
  20.9 38.6 %shard_map.68 = (bf16[2,32,64,128]{3,2,1,0:T(8,128)(2,1)S(1)}, f32[16,16,128]{2,1,0:T(8,128)S(1)}, f32[32,6,128]{2,1,0:T(8,128)S(1)}, bf16[16,256,128]{2,1,0:T(8,128)(2,1)S(1)}) custom-call(s32[32,6]{1,0:T(8,128)S(1)} %fusion.67.slots, s32[32,6]{1,0:T(8,128)S(1)} %copy.58.delays, f32[2,32,6]{2,1,0:T(8,128)S(1)} %copy.59.gains, ...), custom_call_target="tpu_custom_call" | custom-call | tf_op jit(solution)/shard_map/pallas_call | solution.py:353
  59.5 13.5 %shard_map.69 = (f32[256,128]{1,0:T(8,128)S(1)}, f32[4,6,128]{2,1,0:T(8,128)S(1)}) custom-call(f32[256,128]{1,0:T(8,128)S(1)} %bitcast.68, f32[32,6,128]{2,1,0:T(8,128)S(1)} %get-tuple-element.9.cross_ref), custom_call_target="tpu_custom_call" | custom-call | tf_op jit(solution)/shard_map/pallas_call | solution.py:353
  73.3 0.8 slice_multiply_fusion
  74.8 1.2 pad_maximum_fusion.3
  76.0 71.2 %shard_map.70 = f32[4,384,128]{2,1,0:T(8,128)S(1)} custom-call(s32[4,6]{1,0:T(4,128)S(1)} %constant_dynamic-slice_fusion.slots, f32[256,1,128]{2,1,0:T(1,128)S(1)} %bitcast.67, f32[256,1,128]{2,1,0:T(1,128)S(1)} %bitcast.66, f32[4,384,2]{2,1,0:T(8,128)S(1)} %bitcast.65), custom_call_target="tpu_custom_call" | custom-call | tf_op jit(solution)/shard_map/pallas_call | solution.py:353
  147.1 0.7 slice_reduce_fusion.1
  147.9 4.8 %shard_map.71 = f32[8,8,384]{2,1,0:T(8,128)S(1)} custom-call(f32[8,384]{1,0:T(8,128)S(1)} %reshape.182.in_ref), custom_call_target="tpu_custom_call" | custom-call | tf_op jit(solution)/shard_map/pallas_call | solution.py:353
  153.2 7.2 %shard_map.72 = bf16[2,32,64,128]{3,2,1,0:T(8,128)(2,1)S(1)} custom-call(s32[32,6]{1,0:T(8,128)S(1)} %fusion.67.slots, f32[32,6,128]{2,1,0:T(8,128)S(1)} %reshape.197.taps_ref, bf16[16,256,128]{2,1,0:T(8,128)(2,1)S(1)} %get-tuple-element.12.fq_ref, bf16[2,32,64,128]{3,2,1,0:T(8,128)(2,1)S(1)} %get-tuple-element.13.recv_ref), custom_call_target="tpu_custom_call" | custom-call | tf_op jit(solution)/shard_map/pallas_call | solution.py:353
  160.3 1.3 reshape.185
  161.6 0.6 copy.87
  (48 shorter events, 4.0 us)
Async XLA Ops:
  7.3 5.5 %copy-start = (bf16[2,32,8192]{2,1,0:T(8,128)(2,1)S(1)}, bf16[2,32,8192]{2,1,0:T(8,128)(2,1)}, u32[]{:S(2)}) copy-start(bf16[2,32,8192]{2,1,0:T(8,128)(2,1)} %param.9) | copy-start | bytes 3145732
  7.6 5.1 %copy-start.2 = (s32[32,6]{0,1:T(8,128)S(1)}, s32[32,6]{0,1:T(8,128)}, u32[]{:S(2)}) copy-start(s32[32,6]{0,1:T(8,128)} %param.6) | copy-start | bytes 2308
  7.6 10.7 %collective-permute-start = (bf16[8,2,8192]{2,0,1:T(8,128)(2,1)S(1)}, bf16[8,2,8192]{2,0,1:T(8,128)(2,1)S(1)}, u32[]{:S(2)}, u32[]{:S(2)}) collective-permute-start(bf16[8,2,8192]{2,0,1:T(8,128)(2,1)S(1)} %pad_maximum_fusion.1), channel_id=1, source_target_pairs={{0,24},{8,0},{16,8},{24,16},{1,25},{9,1},{17,9},{25,17},{2,26},{10... | collective-permute-start | bytes 786440 | tf_op jit(solution)/shard_map/ppermute | solution.py:23
  12.8 0.7 copy-start.1
  13.5 0.7 copy-start.3
  18.5 2.1 %collective-permute-start.1 = (bf16[16,2,64]{2,0,1:T(8,128)(2,1)S(1)}, bf16[16,2,64]{2,0,1:T(8,128)(2,1)S(1)}, u32[]{:S(2)}, u32[]{:S(2)}) collective-permute-start(bf16[16,2,64]{2,0,1:T(8,128)(2,1)S(1)} %slice.50), channel_id=1, source_target_pairs={{0,1},{1,2},{2,3},{3,4},{4,5},{5,6},{6,7},{8,9},{9,10},{10,11},{11... | collective-permute-start | bytes 12296 | tf_op jit(solution)/shard_map/ppermute | solution.py:29

commit v3 on v2

--- a/solution.py
+++ b/solution.py
@@ -194,7 +194,7 @@
             cross_ref[r, k : k + 1, :] = fold_lags(product)
         return carry
 
-    several(recv_count, 2, receiver)
+    several(recv_count, 4, receiver)
 
 
 def back_kernel(slots, taps_ref, fq_ref, recv_ref, out_ref):
@@ -242,6 +242,33 @@
 
 def as_real(block):
     return jnp.concatenate([block, times_i(block)], axis=0)
+
+
+def three_parts(value):
+    parts = []
+    for _ in range(3):
+        part = value.astype(jnp.bfloat16).astype(jnp.float32)
+        parts.append(part)
+        value = value - part
+    return parts
+
+
+def panel_product(left, rows, place, start):
+    panel = rows.shape[0]
+    for shift in (panel, 2 * panel, 4 * panel):
+        left = left + pltpu.roll(left, shift, 1)
+    high, middle, low = three_parts(left)
+    left = jnp.where(place < 3, high, jnp.where(place < 5, middle, low))
+    left = jnp.where(place < 6, left, 0.0).astype(jnp.bfloat16)
+    gap = jnp.zeros_like(rows)
+    pieces = []
+    for block in (rows, times_i(rows)):
+        p, q, r = three_parts(block)
+        pieces += [p, q, r, p, q, p, gap, gap]
+    turn = start // panel
+    pieces = pieces[len(pieces) - turn :] + pieces[: len(pieces) - turn]
+    right = jnp.concatenate(pieces, axis=0).astype(jnp.bfloat16)
+    return jnp.dot(left, right, preferred_element_type=jnp.float32)
 
 
 def invert(blocks):
@@ -267,12 +294,10 @@
                 rest = rest - col_re * row - col_im * row_i
                 panels[s] = jnp.where(row_id == t, row, rest)
         chosen = group == start // panel
+        place = (lanes_of(blocks[0].shape) + (LANES - start)) % size // panel
         for s, (a, rows) in enumerate(zip(blocks, panels)):
-            above = [jnp.zeros((start, LANES), jnp.float32)] if start > 0 else []
             left = size - panel - start
-            below = [jnp.zeros((left, LANES), jnp.float32)] if left > 0 else []
-            pieces = above + [rows] + below + above + [times_i(rows)] + below
-            change = complex_dot(jnp.where(chosen, a, 0.0), jnp.concatenate(pieces, axis=0))
+            change = panel_product(jnp.where(chosen, a, 0.0), rows, place, start)
             rest = jnp.where(chosen, 0.0, a) - change
             above = [rest[:start]] if start > 0 else []
             below = [rest[start + panel :]] if left > 0 else []
@@ -486,9 +511,17 @@
     tm_index = lax.axis_index("tm")
     window_count = 2 * owned
     recv_count = echoes.shape[1]
+    tails = local_refs[:, :, length - DELAYS :]
     following = passed_along(local_refs, "chan", -1)
     window = jnp.concatenate([local_refs, following], axis=0)
-    previous = from_behind(window[:, :, length - DELAYS :], "tm", 1)
+    route = [
+        (c * tm_count + t, (c - 1) % chan_count * tm_count + t + 1)
+        for c in range(chan_count)
+        for t in range(tm_count - 1)
+    ]
+    previous = jnp.concatenate(
+        [from_behind(tails, "tm", 1), lax.ppermute(tails, ("chan", "tm"), route)], axis=0
+    )
     previous = jnp.pad(previous, ((0, 0), (0, 0), (LANES - DELAYS, 0)))[:, :, None, :]
     x = window.reshape(window_count, 2, rows, LANES)
     xp = jnp.concatenate([previous, x[:, :, :-1]], axis=2).astype(jnp.float32)

time: 163 us -> 164 us (level)
  starting transfers between devices: 6.38 us -> 10.6 us
  Pallas kernels: 135 us -> 131 us
    ppermute x0 -> x1, starting transfers between devices: none -> 7.74 us  [local(): lax.ppermute(tails, ('chan', 'tm'), route)]
    ppermute x1, starting transfers between devices: 5.09 us -> 0.49 us  [passed_along(): lax.ppermute(array, axis, [(i, (i + by) % peers) for i in range(peers)])]
    pallas_call x5, Pallas kernels: 135 us -> 131 us  [kernel_call(): pl.pallas_call(body, out_shape=outs, in_specs=[spec_smem] * len(scalars)...]
    ppermute x1, waiting for transfers between devices: 3.89 us -> 5.63 us  [passed_along(): lax.ppermute(array, axis, [(i, (i + by) % peers) for i in range(peers)])]
  transfers between devices with their start and end apart: 2 -> 3, of which waited for: 2 -> 1; matrix products, arithmetic and copies ran while one was open for 0% -> 0% of each run, Pallas kernels for 0% -> 0%
where the time goes in v3:
time: 164 us
  Pallas kernels  131 us (80%)
  starting transfers between devices  10.6 us (6%)
  local copies, waits for them, and re-layouts  6.65 us (4%)
  waiting for transfers between devices  5.63 us (3%)
  matrix products  4.61 us (3%)
  other arithmetic  3.99 us (2%)
    pallas_call x5, Pallas kernels, kernel_call(): pl.pallas_call(body, out_shape=outs, in_specs=[spec_smem] * len(scalars)...  131 us
    ppermute x1, starting transfers between devices, local(): lax.ppermute(tails, ('chan', 'tm'), route)  7.74 us
    ppermute x1, waiting for transfers between devices, passed_along(): lax.ppermute(array, axis, [(i, (i + by) % peers) for i in range(peers)])  5.63 us
  transfers between devices with their start and end apart: 3, of which 1 were waited for; matrix products, arithmetic and copies ran while one was open for 0% of the time, Pallas kernels for 0%

profile of v3, /device:TPU:0, one launch (start us, length us, event | category | flops | bytes accessed | tf_op | source)
XLA Modules:
  0.0 163.6 jit_solution(5584489642648746250)
XLA Ops:
  0.8 1.2 fusion.8
  2.0 0.5 fusion.19
  2.6 0.5 fusion.15
  3.1 0.5 fusion.3
  3.7 0.5 fusion.2
  4.2 0.6 fusion.25
  4.8 0.6 fusion.29
  5.5 0.6 fusion
  6.5 0.6 fusion.1
  7.6 2.3 %collective-permute-start.1 = (bf16[8,2,64]{2,0,1:T(8,128)(2,1)S(1)}, bf16[8,2,64]{2,0,1:T(8,128)(2,1)S(1)}, u32[]{:S(2)}, u32[]{:S(2)}) collective-permute-start(bf16[8,2,64]{2,0,1:T(8,128)(2,1)S(1)} %fusion.81), channel_id=1, source_target_pairs={{0,1},{1,2},{2,3},{3,4},{4,5},{5,6},{6,7},{8,9},{9,10},{10,11},{11... | collective-permute-start | bytes 6152 | tf_op jit(solution)/shard_map/ppermute | solution.py:29
  10.0 7.7 %collective-permute-start.2 = (bf16[8,2,64]{2,0,1:T(8,128)(2,1)S(1)}, bf16[8,2,64]{2,0,1:T(8,128)(2,1)S(1)}, u32[]{:S(2)}, u32[]{:S(2)}) collective-permute-start(bf16[8,2,64]{2,0,1:T(8,128)(2,1)S(1)} %fusion.81), channel_id=1, source_target_pairs={{0,25},{1,26},{2,27},{3,28},{4,29},{5,30},{6,31},{8,1},{9,2},{10,3... | collective-permute-start | bytes 6152 | tf_op jit(solution)/shard_map/ppermute | solution.py:523
  17.8 0.5 collective-permute-start
  19.4 0.6 copy-done.3
  20.3 5.6 %collective-permute-done = bf16[8,2,8192]{2,0,1:T(8,128)(2,1)S(1)} collective-permute-done((bf16[8,2,8192]{2,0,1:T(8,128)(2,1)S(1)}, bf16[8,2,8192]{2,0,1:T(8,128)(2,1)S(1)}, u32[]{:S(2)}, u32[]{:S(2)}) %collective-permute-start) | collective-permute-done | bytes 262176 | tf_op jit(solution)/shard_map/ppermute | solution.py:23
  26.4 41.7 %shard_map.68 = (bf16[2,32,64,128]{3,2,1,0:T(8,128)(2,1)S(1)}, f32[16,16,128]{2,1,0:T(8,128)S(1)}, f32[32,6,128]{2,1,0:T(8,128)S(1)}, bf16[16,256,128]{2,1,0:T(8,128)(2,1)S(1)}) custom-call(s32[32,6]{1,0:T(8,128)S(1)} %fusion.67.slots, s32[32,6]{1,0:T(8,128)S(1)} %copy.58.delays, f32[2,32,6]{2,1,0:T(8,128)S(1)} %copy.59.gains, ...), custom_call_target="tpu_custom_call" | custom-call | tf_op jit(solution)/shard_map/pallas_call | solution.py:378
  68.1 10.2 %shard_map.69 = (f32[256,128]{1,0:T(8,128)S(1)}, f32[4,6,128]{2,1,0:T(8,128)S(1)}) custom-call(f32[256,128]{1,0:T(8,128)S(1)} %bitcast.68, f32[32,6,128]{2,1,0:T(8,128)S(1)} %get-tuple-element.9.cross_ref), custom_call_target="tpu_custom_call" | custom-call | tf_op jit(solution)/shard_map/pallas_call | solution.py:378
  78.6 0.8 slice_multiply_fusion
  80.1 1.2 pad_maximum_fusion.3
  81.2 67.2 %shard_map.70 = f32[4,384,128]{2,1,0:T(8,128)S(1)} custom-call(s32[4,6]{1,0:T(4,128)S(1)} %constant_dynamic-slice_fusion.slots, f32[256,1,128]{2,1,0:T(1,128)S(1)} %bitcast.67, f32[256,1,128]{2,1,0:T(1,128)S(1)} %bitcast.66, f32[4,384,2]{2,1,0:T(8,128)S(1)} %bitcast.65), custom_call_target="tpu_custom_call" | custom-call | tf_op jit(solution)/shard_map/pallas_call | solution.py:378
  148.5 0.7 slice_reduce_fusion.1
  149.2 4.8 %shard_map.71 = f32[8,8,384]{2,1,0:T(8,128)S(1)} custom-call(f32[8,384]{1,0:T(8,128)S(1)} %reshape.182.in_ref), custom_call_target="tpu_custom_call" | custom-call | tf_op jit(solution)/shard_map/pallas_call | solution.py:378
  154.5 7.2 %shard_map.72 = bf16[2,32,64,128]{3,2,1,0:T(8,128)(2,1)S(1)} custom-call(s32[32,6]{1,0:T(8,128)S(1)} %fusion.67.slots, f32[32,6,128]{2,1,0:T(8,128)S(1)} %reshape.197.taps_ref, bf16[16,256,128]{2,1,0:T(8,128)(2,1)S(1)} %get-tuple-element.12.fq_ref, bf16[2,32,64,128]{3,2,1,0:T(8,128)(2,1)S(1)} %get-tuple-element.13.recv_ref), custom_call_target="tpu_custom_call" | custom-call | tf_op jit(solution)/shard_map/pallas_call | solution.py:378
  161.7 1.3 reshape.185
  162.9 0.6 copy.87
  (50 shorter events, 4.2 us)
Async XLA Ops:
  7.3 11.3 %copy-start = (bf16[2,32,8192]{2,1,0:T(8,128)(2,1)S(1)}, bf16[2,32,8192]{2,1,0:T(8,128)(2,1)}, u32[]{:S(2)}) copy-start(bf16[2,32,8192]{2,1,0:T(8,128)(2,1)} %param.9) | copy-start | bytes 3145732
  7.6 12.5 %collective-permute-start.1 = (bf16[8,2,64]{2,0,1:T(8,128)(2,1)S(1)}, bf16[8,2,64]{2,0,1:T(8,128)(2,1)S(1)}, u32[]{:S(2)}, u32[]{:S(2)}) collective-permute-start(bf16[8,2,64]{2,0,1:T(8,128)(2,1)S(1)} %fusion.81), channel_id=1, source_target_pairs={{0,1},{1,2},{2,3},{3,4},{4,5},{5,6},{6,7},{8,9},{9,10},{10,11},{11... | collective-permute-start | bytes 6152 | tf_op jit(solution)/shard_map/ppermute | solution.py:29
  10.0 10.2 %collective-permute-start.2 = (bf16[8,2,64]{2,0,1:T(8,128)(2,1)S(1)}, bf16[8,2,64]{2,0,1:T(8,128)(2,1)S(1)}, u32[]{:S(2)}, u32[]{:S(2)}) collective-permute-start(bf16[8,2,64]{2,0,1:T(8,128)(2,1)S(1)} %fusion.81), channel_id=1, source_target_pairs={{0,25},{1,26},{2,27},{3,28},{4,29},{5,30},{6,31},{8,1},{9,2},{10,3... | collective-permute-start | bytes 6152 | tf_op jit(solution)/shard_map/ppermute | solution.py:523
  17.8 0.7 copy-start.2
  17.8 8.1 %collective-permute-start = (bf16[8,2,8192]{2,0,1:T(8,128)(2,1)S(1)}, bf16[8,2,8192]{2,0,1:T(8,128)(2,1)S(1)}, u32[]{:S(2)}, u32[]{:S(2)}) collective-permute-start(bf16[8,2,8192]{2,0,1:T(8,128)(2,1)S(1)} %pad_maximum_fusion.1), channel_id=1, source_target_pairs={{0,24},{8,0},{16,8},{24,16},{1,25},{9,1},{17,9},{25,17},{2,26},{10... | collective-permute-start | bytes 786440 | tf_op jit(solution)/shard_map/ppermute | solution.py:23
  18.6 0.7 copy-start.1
  19.3 0.7 copy-start.3

commit v4 on v3

--- a/solution.py
+++ b/solution.py
@@ -194,7 +194,7 @@
             cross_ref[r, k : k + 1, :] = fold_lags(product)
         return carry
 
-    several(recv_count, 4, receiver)
+    several(recv_count, 2, receiver)
 
 
 def back_kernel(slots, taps_ref, fq_ref, recv_ref, out_ref):
@@ -280,19 +280,28 @@
     blocks = list(blocks)
     for start in range(0, size, panel):
         panels = [a[start : start + panel] for a in blocks]
-        for t in range(panel):
+        for t in range(0, panel, 2):
             j = start + t
+            pair = (lane % size == j) | (lane % size == j + 1)
             for s, rows in enumerate(panels):
-                col_re = jnp.broadcast_to(rows[:, j : j + 1], shape)
-                col_im = jnp.broadcast_to(rows[:, size + j : size + j + 1], shape)
-                pivot = 1.0 / col_re[t : t + 1]
-                rest = jnp.where((lane == j) | (lane == size + j), 0.0, rows)
-                row = jnp.where(lane[:1] == j, 1.0, rest[t : t + 1])
-                turned = half_turn(row)
-                row_i = jnp.where(lane[:1] < size, -turned, turned) * pivot
-                row = row * pivot
-                rest = rest - col_re * row - col_im * row_i
-                panels[s] = jnp.where(row_id == t, row, rest)
+                re0, re1, im0, im1 = (
+                    jnp.broadcast_to(rows[:, c : c + 1], shape)
+                    for c in (j, j + 1, size + j, size + j + 1)
+                )
+                a, d = re0[t : t + 1], re1[t + 1 : t + 2]
+                b_re, b_im = re1[t : t + 1], im1[t : t + 1]
+                inverse = 1.0 / (a * d - (b_re * b_re + b_im * b_im))
+                rest = jnp.where(pair, 0.0, rows)
+                row0 = jnp.where(lane[:1] == j, 1.0, rest[t : t + 1])
+                row1 = jnp.where(lane[:1] == j + 1, 1.0, rest[t + 1 : t + 2])
+                row0_i, row1_i = times_i(row0), times_i(row1)
+                new0 = (d * row0 - b_re * row1 - b_im * row1_i) * inverse
+                new0_i = (d * row0_i - b_re * row1_i + b_im * row1) * inverse
+                new1 = (a * row1 - b_re * row0 + b_im * row0_i) * inverse
+                new1_i = (a * row1_i - b_re * row0_i - b_im * row0) * inverse
+                rest = rest - (re0 * new0 + im0 * new0_i) - (re1 * new1 + im1 * new1_i)
+                rest = jnp.where(row_id == t, new0, rest)
+                panels[s] = jnp.where(row_id == t + 1, new1, rest)
         chosen = group == start // panel
         place = (lanes_of(blocks[0].shape) + (LANES - start)) % size // panel
         for s, (a, rows) in enumerate(zip(blocks, panels)):
@@ -511,17 +520,9 @@
     tm_index = lax.axis_index("tm")
     window_count = 2 * owned
     recv_count = echoes.shape[1]
-    tails = local_refs[:, :, length - DELAYS :]
     following = passed_along(local_refs, "chan", -1)
     window = jnp.concatenate([local_refs, following], axis=0)
-    route = [
-        (c * tm_count + t, (c - 1) % chan_count * tm_count + t + 1)
-        for c in range(chan_count)
-        for t in range(tm_count - 1)
-    ]
-    previous = jnp.concatenate(
-        [from_behind(tails, "tm", 1), lax.ppermute(tails, ("chan", "tm"), route)], axis=0
-    )
+    previous = from_behind(window[:, :, length - DELAYS :], "tm", 1)
     previous = jnp.pad(previous, ((0, 0), (0, 0), (LANES - DELAYS, 0)))[:, :, None, :]
     x = window.reshape(window_count, 2, rows, LANES)
     xp = jnp.concatenate([previous, x[:, :, :-1]], axis=2).astype(jnp.float32)

time: 164 us -> 146 us (0.89)
  Pallas kernels: 131 us -> 119 us
  starting transfers between devices: 10.6 us -> 6.38 us
    pallas_call x5, Pallas kernels: 131 us -> 119 us  [kernel_call(): pl.pallas_call(body, out_shape=outs, in_specs=[spec_smem] * len(scalars)...]
    ppermute x1 -> x0, starting transfers between devices: 7.74 us -> none  [local(): lax.ppermute(tails, ('chan', 'tm'), route)]
    ppermute x1, starting transfers between devices: 0.49 us -> 5.09 us  [passed_along(): lax.ppermute(array, axis, [(i, (i + by) % peers) for i in range(peers)])]
    ppermute x1, waiting for transfers between devices: 5.63 us -> 3.89 us  [passed_along(): lax.ppermute(array, axis, [(i, (i + by) % peers) for i in range(peers)])]
  transfers between devices with their start and end apart: 3 -> 2, of which waited for: 1 -> 2; matrix products, arithmetic and copies ran while one was open for 0% -> 1% of each run, Pallas kernels for 0% -> 0%
where the time goes in v4:
time: 146 us
  Pallas kernels  119 us (82%)
  local copies, waits for them, and re-layouts  6.63 us (5%)
  starting transfers between devices  6.38 us (4%)
  matrix products  4.61 us (3%)
  waiting for transfers between devices  4.59 us (3%)
  other arithmetic  3.83 us (3%)
    pallas_call x5, Pallas kernels, kernel_call(): pl.pallas_call(body, out_shape=outs, in_specs=[spec_smem] * len(scalars)...  119 us
    ppermute x1, starting transfers between devices, passed_along(): lax.ppermute(array, axis, [(i, (i + by) % peers) for i in range(peers)])  5.09 us
    ppermute x1, waiting for transfers between devices, passed_along(): lax.ppermute(array, axis, [(i, (i + by) % peers) for i in range(peers)])  3.89 us
  transfers between devices with their start and end apart: 2, of which 2 were waited for; matrix products, arithmetic and copies ran while one was open for 1% of the time, Pallas kernels for 0%

profile of v4, /device:TPU:0, one launch (start us, length us, event | category | flops | bytes accessed | tf_op | source)
XLA Modules:
  0.0 146.2 jit_solution(18199190903283816069)
XLA Ops:
  0.8 1.2 fusion.8
  2.0 0.5 fusion.19
  2.6 0.5 fusion.15
  3.1 0.5 fusion.3
  3.7 0.5 fusion.2
  4.2 0.6 fusion.25
  4.8 0.6 fusion.29
  5.5 0.6 fusion
  6.5 0.6 fusion.1
  7.6 5.1 %collective-permute-start = (bf16[8,2,8192]{2,0,1:T(8,128)(2,1)S(1)}, bf16[8,2,8192]{2,0,1:T(8,128)(2,1)S(1)}, u32[]{:S(2)}, u32[]{:S(2)}) collective-permute-start(bf16[8,2,8192]{2,0,1:T(8,128)(2,1)S(1)} %pad_maximum_fusion.1), channel_id=1, source_target_pairs={{0,24},{8,0},{16,8},{24,16},{1,25},{9,1},{17,9},{25,17},{2,26},{10... | collective-permute-start | bytes 786440 | tf_op jit(solution)/shard_map/ppermute | solution.py:23
  13.6 0.6 copy-done.3
  14.4 3.9 %collective-permute-done = bf16[8,2,8192]{2,0,1:T(8,128)(2,1)S(1)} collective-permute-done((bf16[8,2,8192]{2,0,1:T(8,128)(2,1)S(1)}, bf16[8,2,8192]{2,0,1:T(8,128)(2,1)S(1)}, u32[]{:S(2)}, u32[]{:S(2)}) %collective-permute-start) | collective-permute-done | bytes 262176 | tf_op jit(solution)/shard_map/ppermute | solution.py:23
  18.5 1.3 collective-permute-start.1
  19.9 0.7 collective-permute-done.1
  20.9 38.6 %shard_map.68 = (bf16[2,32,64,128]{3,2,1,0:T(8,128)(2,1)S(1)}, f32[16,16,128]{2,1,0:T(8,128)S(1)}, f32[32,6,128]{2,1,0:T(8,128)S(1)}, bf16[16,256,128]{2,1,0:T(8,128)(2,1)S(1)}) custom-call(s32[32,6]{1,0:T(8,128)S(1)} %fusion.67.slots, s32[32,6]{1,0:T(8,128)S(1)} %copy.58.delays, f32[2,32,6]{2,1,0:T(8,128)S(1)} %copy.59.gains, ...), custom_call_target="tpu_custom_call" | custom-call | tf_op jit(solution)/shard_map/pallas_call | solution.py:387
  59.5 13.5 %shard_map.69 = (f32[256,128]{1,0:T(8,128)S(1)}, f32[4,6,128]{2,1,0:T(8,128)S(1)}) custom-call(f32[256,128]{1,0:T(8,128)S(1)} %bitcast.68, f32[32,6,128]{2,1,0:T(8,128)S(1)} %get-tuple-element.9.cross_ref), custom_call_target="tpu_custom_call" | custom-call | tf_op jit(solution)/shard_map/pallas_call | solution.py:387
  73.3 0.8 slice_multiply_fusion
  74.8 1.2 pad_maximum_fusion.3
  76.0 55.1 %shard_map.70 = f32[4,384,128]{2,1,0:T(8,128)S(1)} custom-call(s32[4,6]{1,0:T(4,128)S(1)} %constant_dynamic-slice_fusion.slots, f32[256,1,128]{2,1,0:T(1,128)S(1)} %bitcast.67, f32[256,1,128]{2,1,0:T(1,128)S(1)} %bitcast.66, f32[4,384,2]{2,1,0:T(8,128)S(1)} %bitcast.65), custom_call_target="tpu_custom_call" | custom-call | tf_op jit(solution)/shard_map/pallas_call | solution.py:387
  131.1 0.7 slice_reduce_fusion.1
  131.9 4.8 %shard_map.71 = f32[8,8,384]{2,1,0:T(8,128)S(1)} custom-call(f32[8,384]{1,0:T(8,128)S(1)} %reshape.182.in_ref), custom_call_target="tpu_custom_call" | custom-call | tf_op jit(solution)/shard_map/pallas_call | solution.py:387
  137.1 7.2 %shard_map.72 = bf16[2,32,64,128]{3,2,1,0:T(8,128)(2,1)S(1)} custom-call(s32[32,6]{1,0:T(8,128)S(1)} %fusion.67.slots, f32[32,6,128]{2,1,0:T(8,128)S(1)} %reshape.197.taps_ref, bf16[16,256,128]{2,1,0:T(8,128)(2,1)S(1)} %get-tuple-element.12.fq_ref, bf16[2,32,64,128]{3,2,1,0:T(8,128)(2,1)S(1)} %get-tuple-element.13.recv_ref), custom_call_target="tpu_custom_call" | custom-call | tf_op jit(solution)/shard_map/pallas_call | solution.py:387
  144.3 1.3 reshape.185
  145.6 0.6 copy.87
  (48 shorter events, 4.0 us)
Async XLA Ops:
  7.3 5.5 %copy-start = (bf16[2,32,8192]{2,1,0:T(8,128)(2,1)S(1)}, bf16[2,32,8192]{2,1,0:T(8,128)(2,1)}, u32[]{:S(2)}) copy-start(bf16[2,32,8192]{2,1,0:T(8,128)(2,1)} %param.9) | copy-start | bytes 3145732
  7.6 5.1 %copy-start.2 = (s32[32,6]{0,1:T(8,128)S(1)}, s32[32,6]{0,1:T(8,128)}, u32[]{:S(2)}) copy-start(s32[32,6]{0,1:T(8,128)} %param.6) | copy-start | bytes 2308
  7.6 10.7 %collective-permute-start = (bf16[8,2,8192]{2,0,1:T(8,128)(2,1)S(1)}, bf16[8,2,8192]{2,0,1:T(8,128)(2,1)S(1)}, u32[]{:S(2)}, u32[]{:S(2)}) collective-permute-start(bf16[8,2,8192]{2,0,1:T(8,128)(2,1)S(1)} %pad_maximum_fusion.1), channel_id=1, source_target_pairs={{0,24},{8,0},{16,8},{24,16},{1,25},{9,1},{17,9},{25,17},{2,26},{10... | collective-permute-start | bytes 786440 | tf_op jit(solution)/shard_map/ppermute | solution.py:23
  12.8 0.7 copy-start.1
  13.5 0.7 copy-start.3
  18.5 2.1 %collective-permute-start.1 = (bf16[16,2,64]{2,0,1:T(8,128)(2,1)S(1)}, bf16[16,2,64]{2,0,1:T(8,128)(2,1)S(1)}, u32[]{:S(2)}, u32[]{:S(2)}) collective-permute-start(bf16[16,2,64]{2,0,1:T(8,128)(2,1)S(1)} %slice.50), channel_id=1, source_target_pairs={{0,1},{1,2},{2,3},{3,4},{4,5},{5,6},{6,7},{8,9},{9,10},{10,11},{11... | collective-permute-start | bytes 12296 | tf_op jit(solution)/shard_map/ppermute | solution.py:29

commit v5 on v4

--- a/solution.py
+++ b/solution.py
@@ -169,7 +169,7 @@
             corr_ref[j, i : i + 1, :] = fold_lags(product)
         return carry
 
-    lax.fori_loop(0, window, pairs, 0)
+    several(window, 2, pairs)
 
     def receiver(r, carry):
         re = jnp.zeros((rows, LANES), jnp.float32)

time: 146 us -> 141 us (0.966)
  Pallas kernels: 119 us -> 114 us
    pallas_call x5, Pallas kernels: 119 us -> 114 us  [kernel_call(): pl.pallas_call(body, out_shape=outs, in_specs=[spec_smem] * len(scalars)...]
where the time goes in v5:
time: 141 us
  Pallas kernels  114 us (81%)
  local copies, waits for them, and re-layouts  6.63 us (5%)
  starting transfers between devices  6.38 us (5%)
  matrix products  4.61 us (3%)
  waiting for transfers between devices  4.59 us (3%)
  other arithmetic  3.83 us (3%)
    pallas_call x5, Pallas kernels, kernel_call(): pl.pallas_call(body, out_shape=outs, in_specs=[spec_smem] * len(scalars)...  114 us
    ppermute x1, starting transfers between devices, passed_along(): lax.ppermute(array, axis, [(i, (i + by) % peers) for i in range(peers)])  5.09 us
    ppermute x1, waiting for transfers between devices, passed_along(): lax.ppermute(array, axis, [(i, (i + by) % peers) for i in range(peers)])  3.89 us
  transfers between devices with their start and end apart: 2, of which 2 were waited for; matrix products, arithmetic and copies ran while one was open for 1% of the time, Pallas kernels for 0%

profile of v5, /device:TPU:0, one launch (start us, length us, event | category | flops | bytes accessed | tf_op | source)
XLA Modules:
  0.0 140.8 jit_solution(8729445798630177358)
XLA Ops:
  0.8 1.2 fusion.8
  2.0 0.5 fusion.19
  2.6 0.5 fusion.15
  3.1 0.5 fusion.3
  3.7 0.5 fusion.2
  4.2 0.6 fusion.25
  4.8 0.6 fusion.29
  5.5 0.6 fusion
  6.5 0.6 fusion.1
  7.6 5.1 %collective-permute-start = (bf16[8,2,8192]{2,0,1:T(8,128)(2,1)S(1)}, bf16[8,2,8192]{2,0,1:T(8,128)(2,1)S(1)}, u32[]{:S(2)}, u32[]{:S(2)}) collective-permute-start(bf16[8,2,8192]{2,0,1:T(8,128)(2,1)S(1)} %pad_maximum_fusion.1), channel_id=1, source_target_pairs={{0,24},{8,0},{16,8},{24,16},{1,25},{9,1},{17,9},{25,17},{2,26},{10... | collective-permute-start | bytes 786440 | tf_op jit(solution)/shard_map/ppermute | solution.py:23
  13.6 0.6 copy-done.3
  14.4 3.9 %collective-permute-done = bf16[8,2,8192]{2,0,1:T(8,128)(2,1)S(1)} collective-permute-done((bf16[8,2,8192]{2,0,1:T(8,128)(2,1)S(1)}, bf16[8,2,8192]{2,0,1:T(8,128)(2,1)S(1)}, u32[]{:S(2)}, u32[]{:S(2)}) %collective-permute-start) | collective-permute-done | bytes 262176 | tf_op jit(solution)/shard_map/ppermute | solution.py:23
  18.5 1.3 collective-permute-start.1
  19.9 0.7 collective-permute-done.1
  20.9 33.1 %shard_map.68 = (bf16[2,32,64,128]{3,2,1,0:T(8,128)(2,1)S(1)}, f32[16,16,128]{2,1,0:T(8,128)S(1)}, f32[32,6,128]{2,1,0:T(8,128)S(1)}, bf16[16,256,128]{2,1,0:T(8,128)(2,1)S(1)}) custom-call(s32[32,6]{1,0:T(8,128)S(1)} %fusion.67.slots, s32[32,6]{1,0:T(8,128)S(1)} %copy.58.delays, f32[2,32,6]{2,1,0:T(8,128)S(1)} %copy.59.gains, ...), custom_call_target="tpu_custom_call" | custom-call | tf_op jit(solution)/shard_map/pallas_call | solution.py:387
  54.0 13.5 %shard_map.69 = (f32[256,128]{1,0:T(8,128)S(1)}, f32[4,6,128]{2,1,0:T(8,128)S(1)}) custom-call(f32[256,128]{1,0:T(8,128)S(1)} %bitcast.68, f32[32,6,128]{2,1,0:T(8,128)S(1)} %get-tuple-element.9.cross_ref), custom_call_target="tpu_custom_call" | custom-call | tf_op jit(solution)/shard_map/pallas_call | solution.py:387
  67.9 0.8 slice_multiply_fusion
  69.3 1.2 pad_maximum_fusion.3
  70.5 55.1 %shard_map.70 = f32[4,384,128]{2,1,0:T(8,128)S(1)} custom-call(s32[4,6]{1,0:T(4,128)S(1)} %constant_dynamic-slice_fusion.slots, f32[256,1,128]{2,1,0:T(1,128)S(1)} %bitcast.67, f32[256,1,128]{2,1,0:T(1,128)S(1)} %bitcast.66, f32[4,384,2]{2,1,0:T(8,128)S(1)} %bitcast.65), custom_call_target="tpu_custom_call" | custom-call | tf_op jit(solution)/shard_map/pallas_call | solution.py:387
  125.7 0.7 slice_reduce_fusion.1
  126.4 4.8 %shard_map.71 = f32[8,8,384]{2,1,0:T(8,128)S(1)} custom-call(f32[8,384]{1,0:T(8,128)S(1)} %reshape.182.in_ref), custom_call_target="tpu_custom_call" | custom-call | tf_op jit(solution)/shard_map/pallas_call | solution.py:387
  131.7 7.2 %shard_map.72 = bf16[2,32,64,128]{3,2,1,0:T(8,128)(2,1)S(1)} custom-call(s32[32,6]{1,0:T(8,128)S(1)} %fusion.67.slots, f32[32,6,128]{2,1,0:T(8,128)S(1)} %reshape.197.taps_ref, bf16[16,256,128]{2,1,0:T(8,128)(2,1)S(1)} %get-tuple-element.12.fq_ref, bf16[2,32,64,128]{3,2,1,0:T(8,128)(2,1)S(1)} %get-tuple-element.13.recv_ref), custom_call_target="tpu_custom_call" | custom-call | tf_op jit(solution)/shard_map/pallas_call | solution.py:387
  138.8 1.3 reshape.185
  140.1 0.6 copy.87
  (48 shorter events, 4.0 us)
Async XLA Ops:
  7.3 5.5 %copy-start = (bf16[2,32,8192]{2,1,0:T(8,128)(2,1)S(1)}, bf16[2,32,8192]{2,1,0:T(8,128)(2,1)}, u32[]{:S(2)}) copy-start(bf16[2,32,8192]{2,1,0:T(8,128)(2,1)} %param.9) | copy-start | bytes 3145732
  7.6 5.1 %copy-start.2 = (s32[32,6]{0,1:T(8,128)S(1)}, s32[32,6]{0,1:T(8,128)}, u32[]{:S(2)}) copy-start(s32[32,6]{0,1:T(8,128)} %param.6) | copy-start | bytes 2308
  7.6 10.7 %collective-permute-start = (bf16[8,2,8192]{2,0,1:T(8,128)(2,1)S(1)}, bf16[8,2,8192]{2,0,1:T(8,128)(2,1)S(1)}, u32[]{:S(2)}, u32[]{:S(2)}) collective-permute-start(bf16[8,2,8192]{2,0,1:T(8,128)(2,1)S(1)} %pad_maximum_fusion.1), channel_id=1, source_target_pairs={{0,24},{8,0},{16,8},{24,16},{1,25},{9,1},{17,9},{25,17},{2,26},{10... | collective-permute-start | bytes 786440 | tf_op jit(solution)/shard_map/ppermute | solution.py:23
  12.8 0.7 copy-start.1
  13.5 0.7 copy-start.3
  18.5 2.1 %collective-permute-start.1 = (bf16[16,2,64]{2,0,1:T(8,128)(2,1)S(1)}, bf16[16,2,64]{2,0,1:T(8,128)(2,1)S(1)}, u32[]{:S(2)}, u32[]{:S(2)}) collective-permute-start(bf16[16,2,64]{2,0,1:T(8,128)(2,1)S(1)} %slice.50), channel_id=1, source_target_pairs={{0,1},{1,2},{2,3},{3,4},{4,5},{5,6},{6,7},{8,9},{9,10},{10,11},{11... | collective-permute-start | bytes 12296 | tf_op jit(solution)/shard_map/ppermute | solution.py:29
